TPU v7x, 128 devices: a whole 4x4x4 slice. The times are simulated.
128 devices in a mesh: rep: 32 (over y, x, z_hi), shard: 4 (over z_lo, core).
Axes of the slice: x: 4, y: 4, z: 4 (z_hi: 2, z_lo: 2; z = z_hi * 2 + z_lo), core: 2. Of those that a mesh axis runs over, the one named last changes fastest.
Arguments:
- partials: bfloat16 [32, 4, 192, 28672], P('rep', 'shard'), may hold values from -6 to 6
- momentum: float32 [32, 192, 28672], P('rep', None, 'shard'), may hold values from -6 to 6
- weight: bfloat16 [192, 28672], P(None, 'shard'), may hold values from -6 to 6
- kept: int32 [6, 896, 64], P(None, 'shard'), may hold values from 0 to 495, as said below
Outputs:
- new_momentum: float32 [32, 192, 28672], P('rep', None, 'shard')
- aggregate: float32 [192, 28672], P(None, 'shard')
- new_weight: bfloat16 [192, 28672], P(None, 'shard')
Inputs may be any that keep to these rules, and one draw needn't show every extreme that they name: `kept`: within each block the 64 positions are distinct, and each is 32 k + l with k and l below 16 (the positions are fixed in advance and shared by all replicas, a simplification of DeMo's per-replica top-k).
All inputs are finite; a program needn't handle non-finite values.
Results may differ from a plain program's by a relative error of at most 0.001.
Values sent between devices are 32-bit elements; how exact they have to be, the bound alone decides.
A program may use at most 192 MiB of HBM per device.

v0:
```python
import jax
import jax.numpy as jnp
from jax import lax
from jax.sharding import PartitionSpec as P

decay_rate = 0.9
step_rate = 0.5


def dct_low():
    freq = jnp.arange(16, dtype=jnp.float32)[:, None]
    place_idx = jnp.arange(32, dtype=jnp.float32)[None, :]
    table = jnp.cos(jnp.pi * (2.0 * place_idx + 1.0) * freq / 64.0) * jnp.sqrt(
        jnp.float32(2.0 / 32.0)
    )
    return jnp.where(freq == 0.0, table * jnp.sqrt(jnp.float32(0.5)), table)


def selector(kept_band):
    corner_pos = kept_band // 32 * 16 + kept_band % 32
    return (corner_pos[:, :, None] == jnp.arange(256, dtype=jnp.int32)[None, None, :]).astype(
        jnp.float32
    )


def corners_of(band_data, low_table, block_table):
    count, height, width_cols = band_data.shape
    lefted = jnp.einsum("ki,biw->bkw", low_table, band_data, precision=lax.Precision.HIGHEST)
    righted = jnp.dot(lefted.reshape(-1, 256), block_table, precision=lax.Precision.HIGHEST)
    blocks = width_cols // 32
    righted = righted.reshape(count, 16, blocks, 16).transpose(0, 2, 1, 3)
    return righted.reshape(count, blocks, 256)


def compress(reduced, moment_in, kept_part, low_table, block_table):
    total_rows, width_cols = reduced.shape
    moment = decay_rate * moment_in + reduced
    corners = corners_of(moment.reshape(total_rows // 32, 32, width_cols), low_table, block_table)
    picked = []
    for band_index in range(total_rows // 32):
        chosen = jnp.einsum(
            "cjq,cq->cj",
            selector(kept_part[band_index]),
            corners[band_index],
            precision=lax.Precision.HIGHEST,
        )
        picked.append(chosen.reshape(1, -1))
    return (moment, jnp.concatenate(picked, axis=0))


def expand_both(stacked, kept, low_table, block_table, width_cols):
    pairs, count, flat_count = stacked.shape
    blocks = width_cols // 32
    values = stacked.reshape(pairs, count, blocks, 64)
    placed = []
    for band_index in range(count):
        placed.append(
            jnp.einsum(
                "cjq,scj->scq",
                selector(kept[band_index]),
                values[:, band_index],
                precision=lax.Precision.HIGHEST,
            )
        )
    corners = (
        jnp.stack(placed, axis=1).reshape(pairs, count, blocks, 16, 16).transpose(0, 1, 3, 2, 4)
    )
    righted = jnp.dot(corners.reshape(-1, 128), block_table.T, precision=lax.Precision.HIGHEST)
    righted = righted.reshape(pairs, count, 16, width_cols)
    return jnp.einsum("ki,sbkw->sbiw", low_table, righted, precision=lax.Precision.HIGHEST)


def per_device(partials, momentum, weight, kept):
    low_table = dct_low()
    block_table = jnp.kron(jnp.eye(8, dtype=jnp.float32), low_table.T)
    partial_rows = partials.reshape(partials.shape[2], partials.shape[3]).astype(jnp.float32)
    moment_in = momentum.reshape(momentum.shape[1], momentum.shape[2])
    total_rows, width_cols = moment_in.shape
    reduced = lax.psum_scatter(partial_rows, "shard", scatter_dimension=1, tiled=True)
    moment, sent = compress(reduced, moment_in, kept, low_table, block_table)
    summed = lax.psum(sent, "rep")
    mean_sent = summed / lax.axis_size("rep")
    expanded = expand_both(
        jnp.stack([sent, mean_sent], axis=0), kept, low_table, block_table, width_cols
    )
    estimate = expanded[0].reshape(total_rows, width_cols)
    aggregate = expanded[1].reshape(total_rows, width_cols)
    new_momentum = (moment - estimate).reshape(1, total_rows, width_cols)
    new_weight = (weight.astype(jnp.float32) - step_rate * aggregate).astype(jnp.bfloat16)
    return (new_momentum, aggregate, new_weight)


def solution(mesh):
    placed = (
        P("rep", "shard", None, None),
        P("rep", None, "shard"),
        P(None, "shard"),
        P(None, "shard", None),
    )
    return jax.shard_map(
        per_device,
        mesh=mesh,
        in_specs=placed,
        out_specs=(P("rep", None, "shard"), P(None, "shard"), P(None, "shard")),
        check_vma=False,
    )
```

profile of v0, /device:TPU:0, one launch (start us, length us, event | category | flops | bytes accessed | tf_op | source)
XLA Modules:
  0.0 780.3 jit_solution(17908139850253841928)
XLA Ops:
  7.2 12.1 %bitcast_convert_fusion = f32[192,28672]{1,0:T(8,128)} fusion(bf16[1,1,192,28672]{3,2,1,0:T(8,128)(2,1)} %param.4), kind=kLoop, calls=%fused_computation.18 | loop fusion | flops 5505024 | bytes 33030144 | tf_op jit(solution)/shard_map/convert_element_type | solution.py:76
  19.4 0.9 copy-done.6
  24.9 185.9 %reduce-scatter.2.cloned.1.call-done = f32[192,7168]{1,0:T(8,128)} async-done(((f32[192,28672]{1,0:T(8,128)}), f32[192,7168]{1,0:T(8,128)}) %reduce-scatter.2.cloned.1.call-update) | async-done | bytes 5505040 | tf_op jit(solution)/shard_map/reduce_scatter | solution.py:79
  210.8 4.9 bitcast_add_fusion
  215.7 2.4 copy-done
  218.1 4.7 convolution_bitcast_fusion.1
  222.8 3.2 reshape.470
  226.0 3.4 fusion.117
  229.4 7.4 reshape.471
  236.9 7.9 %fusion.116 = (f32[1,224,16,16]{3,1,2,0:T(8,128)}, f32[1,224,16,16]{3,1,2,0:T(8,128)}, f32[1,224,16,16]{3,1,2,0:T(8,128)}, f32[1,224,16,16]{3,1,2,0:T(8,128)}, f...) fusion(f32[6,224,16,16]{3,1,2,0:T(8,128)} %bitcast.251), kind=kLoop, calls=%fused_computation.194 | loop fusion | bytes 2752512 | tf_op jit(solution)/shard_map/slice | solution.py:44
  244.8 2.1 copy.24
  247.0 2.1 copy.22
  249.2 2.1 copy.20
  251.5 2.1 copy.18
  253.7 2.1 copy.16
  256.7 8.7 %bitcast_dynamic-update-slice_fusion.5 = (f32[1,6,224,64]{3,0,2,1:T(1,128)S(1)}, f32[224,1,64]{2,1,0:T(1,128)S(1)}) fusion(f32[224,256,1]{1,2,0:T(1,128)S(1)} %copy.33, s32[224,64]{1,0:T(8,128)} %copy.13), kind=kOutput, calls=%fused_computation.72 | convolution fusion | flops 47710208 | bytes 516096 | tf_op jit(solution)/shard_map/cjq,cq->cj/dot_general | solution.py:41
  265.4 8.0 %bitcast_dynamic-update-slice_fusion.4 = (f32[1,6,224,64]{3,0,2,1:T(1,128)S(1)}, f32[224,1,64]{2,1,0:T(1,128)S(1)}) fusion(f32[1,6,224,64]{3,0,2,1:T(1,128)S(1)} %get-tuple-element.17, f32[224,256,1]{1,2,0:T(1,128)S(1)} %copy.35, s32[224,64]{1,0:T(8,128)S(1)} %copy-done.11), kind=kOutput, calls=%fused_computation.71 | convolution fusion | flops 47710208 | bytes 573440 | tf_op jit(solution)/shard_map/cjq,cq->cj/dot_general | solution.py:41
  273.3 8.0 %bitcast_dynamic-update-slice_fusion.3 = (f32[1,6,224,64]{3,0,2,1:T(1,128)S(1)}, f32[224,1,64]{2,1,0:T(1,128)S(1)}) fusion(f32[1,6,224,64]{3,0,2,1:T(1,128)S(1)} %get-tuple-element.19, f32[224,256,1]{1,2,0:T(1,128)S(1)} %copy.37, s32[224,64]{1,0:T(8,128)S(1)} %copy-done.8), kind=kOutput, calls=%fused_computation.70 | convolution fusion | flops 47710208 | bytes 573440 | tf_op jit(solution)/shard_map/cjq,cq->cj/dot_general | solution.py:41
  281.3 8.0 %bitcast_dynamic-update-slice_fusion.2 = (f32[1,6,224,64]{3,0,2,1:T(1,128)S(1)}, f32[224,1,64]{2,1,0:T(1,128)S(1)}) fusion(f32[1,6,224,64]{3,0,2,1:T(1,128)S(1)} %get-tuple-element.21, f32[224,256,1]{1,2,0:T(1,128)S(1)} %copy.39, s32[224,64]{1,0:T(8,128)S(1)} %copy-done.7), kind=kOutput, calls=%fused_computation.69 | convolution fusion | flops 47710208 | bytes 573440 | tf_op jit(solution)/shard_map/cjq,cq->cj/dot_general | solution.py:41
  289.3 8.0 %bitcast_dynamic-update-slice_fusion.1 = (f32[1,6,224,64]{3,0,2,1:T(1,128)S(1)}, f32[224,1,64]{2,1,0:T(1,128)S(1)}) fusion(f32[1,6,224,64]{3,0,2,1:T(1,128)S(1)} %get-tuple-element.23, f32[224,256,1]{1,2,0:T(1,128)S(1)} %copy.41, s32[224,64]{1,0:T(8,128)S(1)} %copy-done.10), kind=kOutput, calls=%fused_computation.68 | convolution fusion | flops 47710208 | bytes 573440 | tf_op jit(solution)/shard_map/cjq,cq->cj/dot_general | solution.py:41
  297.2 8.1 %bitcast_dynamic-update-slice_fusion = (f32[1,6,224,64]{3,0,2,1:T(1,128)S(1)}, f32[224,1,64]{2,1,0:T(1,128)S(1)}) fusion(f32[1,6,224,64]{3,0,2,1:T(1,128)S(1)} %get-tuple-element.25, f32[224,256,1]{1,2,0:T(1,128)S(1)} %copy.43, s32[224,64]{1,0:T(8,128)S(1)} %copy.23), kind=kOutput, calls=%fused_computation.67 | convolution fusion | flops 47710208 | bytes 573440 | tf_op jit(solution)/shard_map/cjq,cq->cj/dot_general | solution.py:41
  306.1 1.2 concatenate.27
  307.4 346.0 %all-reduce.2.cloned.1.call-done = f32[6,14336]{1,0:T(8,128)} async-done(((f32[6,14336]{1,0:T(8,128)}), f32[6,14336]{1,0:T(8,128)}) %all-reduce.2.cloned.1.call-update) | async-done | bytes 344080 | tf_op jit(solution)/shard_map/psum | solution.py:81
  653.3 1.1 broadcast_multiply_fusion.1
  654.7 6.2 fusion.24
  660.9 6.1 fusion.25
  667.0 6.1 fusion.26
  673.1 6.1 fusion.27
  679.2 6.1 fusion.29
  685.3 6.7 fusion.28
  692.0 1.0 copy.26
  693.0 1.0 copy.27
  694.1 1.0 copy.28
  695.1 1.0 copy.29
  696.1 1.0 copy.30
  697.1 1.0 copy.31
  698.2 1.2 constant_dynamic-update-slice_fusion.5
  699.3 1.1 constant_dynamic-update-slice_fusion.4
  700.4 1.1 constant_dynamic-update-slice_fusion.3
  701.5 1.1 constant_dynamic-update-slice_fusion.2
  702.7 10.5 %copy.32 = f32[2,6,16,224,16]{4,3,2,1,0:T(8,128)} copy(f32[2,6,16,224,16]{3,4,2,0,1:T(8,128)S(1)} %bitcast.254) | data formatting | bytes 5505024 | tf_op jit(solution)/shard_map/transpose | solution.py:66
  713.2 13.2 %reshape.478 = f32[5376,128]{1,0:T(8,128)S(1)} reshape(f32[2,6,16,224,16]{4,3,2,1,0:T(8,128)} %copy.32) | data formatting | bytes 5505024 | tf_op jit(solution)/shard_map/reshape | solution.py:68
  726.4 6.2 fusion.118
  732.5 7.2 reshape.479
  739.7 15.4 %convolution_bitcast_fusion = f32[2,6,32,7168]{3,2,1,0:T(8,128)} fusion(f32[2,6,16,7168]{3,2,1,0:T(8,128)} %reshape.479, f32[32]{0:T(128)S(1)} %add_multiply_fusion, pred[16]{0:T(512)(128)(4,1)S(1)} %iota_compare_fusion.31), kind=kOutput, calls=%fused_computation.19 | convolution fusion | flops 528484864 | bytes 16515216 | tf_op jit(solution)/shard_map/ki,sbkw->sbiw/dot_general | solution.py:70
  755.1 7.9 %fusion.115 = (f32[1,6,32,7168]{3,2,1,0:T(8,128)S(1)}, f32[1,6,32,7168]{3,2,1,0:T(8,128)}) fusion(f32[2,6,32,7168]{3,2,1,0:T(8,128)} %convolution_bitcast_fusion), kind=kLoop, calls=%fused_computation.193 | loop fusion | bytes 22020096 | tf_op jit(solution)/shard_map/slice | solution.py:87
  763.0 7.8 bitcast_subtract_fusion
  770.8 2.4 subtract_convert_fusion
  (68 shorter events, 7.3 us)
Async XLA Ops:
  7.2 203.7 %reduce-scatter.2.cloned.1.call-start = ((), (), s32[]{:S(2)}) async-start(), calls=%async_computation.1 | async-start | bytes 27525120 | tf_op jit(solution)/shard_map/reduce_scatter | solution.py:79
  19.4 1.0 copy-start.6
  19.4 634.0 %all-reduce.2.cloned.1.call-start = ((), (), s32[]{:S(2)}) async-start(), calls=%async_computation.2 | async-start | bytes 917504 | tf_op jit(solution)/shard_map/psum | solution.py:81
  215.7 2.4 copy-start
  256.6 8.7 %copy-start.11 = (s32[224,64]{1,0:T(8,128)S(1)}, s32[224,64]{1,0:T(8,128)}, u32[]{:S(2)}) copy-start(s32[224,64]{1,0:T(8,128)} %copy.15) | copy-start | bytes 172036
  265.3 8.0 %copy-start.8 = (s32[224,64]{1,0:T(8,128)S(1)}, s32[224,64]{1,0:T(8,128)}, u32[]{:S(2)}) copy-start(s32[224,64]{1,0:T(8,128)} %copy.17) | copy-start | bytes 172036
  273.3 8.0 %copy-start.7 = (s32[224,64]{1,0:T(8,128)S(1)}, s32[224,64]{1,0:T(8,128)}, u32[]{:S(2)}) copy-start(s32[224,64]{1,0:T(8,128)} %copy.19) | copy-start | bytes 172036
  281.3 8.0 %copy-start.10 = (s32[224,64]{1,0:T(8,128)S(1)}, s32[224,64]{1,0:T(8,128)}, u32[]{:S(2)}) copy-start(s32[224,64]{1,0:T(8,128)} %copy.21) | copy-start | bytes 172036
  305.3 348.0 %copy-start.14 = (f32[1,6,224,64]{3,0,2,1:T(1,128)}, f32[1,6,224,64]{3,0,2,1:T(1,128)S(1)}, u32[]{:S(2)}) copy-start(f32[1,6,224,64]{3,0,2,1:T(1,128)S(1)} %get-tuple-element.27) | copy-start | bytes 1032196
  305.3 349.3 %copy-start.13 = (s32[224,64]{1,0:T(8,128)S(1)}, s32[224,64]{1,0:T(8,128)}, u32[]{:S(2)}) copy-start(s32[224,64]{1,0:T(8,128)} %copy.13) | copy-start | bytes 172036
  654.7 6.2 copy-start.12
  654.7 6.2 copy-start.15
  660.9 6.1 copy-start.9
  692.0 4.1 copy-start.5
  698.1 4.4 copy-start.4
  698.2 4.5 copy-start.3
  739.7 23.3 %slice-start = ((s8[5505024]{0:T(1024)(128)(4,1)}), s8[4194304]{0:T(1024)(128)(4,1)S(1)}, s32[]{:S(2)}) async-start(s8[5505024]{0:T(1024)(128)(4,1)} %bitcast.249), calls=%async_computation.3 | async-start | bytes 8388608
  755.1 7.9 %slice-start.1 = ((s8[5505024]{0:T(1024)(128)(4,1)}), s8[1310720]{0:T(1024)(128)(4,1)S(1)}, s32[]{:S(2)}) async-start(s8[5505024]{0:T(1024)(128)(4,1)} %bitcast.249), calls=%async_computation.4 | async-start | bytes 2621440
  763.0 7.8 copy-start.1
  763.0 7.8 copy-start.2
Sparse Core Ops, SparseCore 0:
  19.5 191.2 reduce-scatter.1
  307.5 345.8 all-reduce.1
where the time goes:
time: 786 us; the launch traced here: 780 us
  waiting for transfers between devices  532 us (68%)
  matrix products  115 us (15%)
  local copies, waits for them, and re-layouts  89.4 us (11%)
  other arithmetic  28.8 us (4%)
  between operations  14.7 us (2%)
    psum x1, waiting for transfers between devices, per_device(): summed = lax.psum(sent, 'rep')  346 us
    reduce_scatter x1, waiting for transfers between devices, per_device(): lax.psum_scatter(partial_rows, 'shard', scatter_dimension=1, tiled=True)  186 us
    dot_general x6, matrix products, compress(): jnp.einsum('cjq,cq->cj', selector(kept_part[band_index]), corners[band_in...  48.6 us
    dot_general x6, matrix products, expand_both(): jnp.einsum('cjq,scj->scq', selector(kept[band_index]), values[:, band_ind...  37.3 us
    slice x7, local copies, waits for them, and re-layouts, compress(): corners[band_index]  18.8 us
  transfers between devices with their start and end apart: 2, of which 2 were waited for; matrix products, arithmetic and copies ran while one was open for 1% of the time, Pallas kernels for 0%

commit v1 on v0

v1 whole, which is shorter than its diff:
```python
import functools

import jax
import jax.numpy as jnp
import numpy as np
from jax import lax
from jax.experimental import pallas as pl
from jax.experimental.pallas import tpu as pltpu
from jax.sharding import PartitionSpec as P

decay_rate = 0.9
step_rate = 0.5

MESH = pl.DeviceIdType.MESH
ROWS = 192
LOW = 96
CHUNK = 512
CHUNKS = 14
GROUPS = 7
QUARTER = CHUNK * CHUNKS
SLOTS = 4
PIECE = 24


def low_tables():
    freq = np.arange(16, dtype=np.float64)[:, None]
    place = np.arange(32, dtype=np.float64)[None, :]
    low = np.cos(np.pi * (2.0 * place + 1.0) * freq / 64.0) * np.sqrt(2.0 / 32.0)
    low[0] *= np.sqrt(0.5)
    left = np.kron(np.eye(6), low)
    right = np.kron(np.eye(8), low.T)

    def split(table):
        table = table.astype(np.float32)
        high = table.astype(jnp.bfloat16)
        rest = (table - high.astype(np.float32)).astype(jnp.bfloat16)
        return np.stack([high, rest])

    return split(left), split(right), split(left.T.copy()), split(right.T.copy())


def split_dot(a, b):
    if isinstance(a, tuple):
        a_high, a_rest = a
        b_high = b.astype(jnp.bfloat16)
        b_rest = (b - b_high.astype(jnp.float32)).astype(jnp.bfloat16)
    else:
        b_high, b_rest = b
        a_high = a.astype(jnp.bfloat16)
        a_rest = (a - a_high.astype(jnp.float32)).astype(jnp.bfloat16)
    dot = functools.partial(jnp.dot, preferred_element_type=jnp.float32)
    return dot(a_high, b_high) + (dot(a_high, b_rest) + dot(a_rest, b_high))


def kernel(part, mom, wt, kept, left_in, right_in, left_t_in, right_t_in,
           moment_out, agg_out, weight_out,
           pbuf, stage, sib, zrecv, mombuf, wbuf, cf, rsr, red, z3r, mean, mask, keptb, rowbits,
           left, right, left_t, right_t,
           const_sem, p_sem, m_sem, w_sem, ss_sem, sr_sem, zs_sem, zr_sem,
           rs_s, rs_r, z3_s, z3_r, ag_s, ag_r, om_sem, oa_sem, ow_sem):
    f32 = jnp.float32
    rep, shard = lax.axis_index("rep"), lax.axis_index("shard")
    plane, z_hi = rep // 2, rep % 2
    y, x = plane // 4, plane % 4
    z_lo, core = shard // 2, shard % 2
    z = z_hi * 2 + z_lo

    def in_plane(k):
        py, px = (y + k // 4) % 4, (x + k % 4) % 4
        return py, px, ((py * 4 + px) * 2 + z_hi, shard)

    def along_z(dz):
        other = (z + dz) % 4
        return (plane * 2 + other // 2, (other % 2) * 2 + core)

    sibling = (rep, z_lo * 2 + (1 - core))
    partner = (rep, (1 - z_lo) * 2 + core)
    quarters = ((1 - z_lo) * 2 + (1 - core), z_lo * 2 + (1 - core), (1 - z_lo) * 2 + core, shard)

    def load_part(c):
        return [
            pltpu.make_async_copy(
                part.at[0, 0, :, pl.ds(pl.multiple_of(q * QUARTER + c * CHUNK, CHUNK), CHUNK)],
                pbuf.at[c, n], p_sem.at[c])
            for n, q in enumerate(quarters)
        ]

    def columns(c):
        return pl.ds(pl.multiple_of(c * CHUNK, CHUNK), CHUNK)

    def load_mom(c):
        return pltpu.make_async_copy(mom.at[0, :, columns(c)], mombuf.at[c], m_sem.at[c])

    def load_weight(c):
        return pltpu.make_async_copy(wt.at[:, columns(c)], wbuf.at[c], w_sem.at[c])

    consts = [
        pltpu.make_async_copy(src, dst, const_sem.at[n])
        for n, (src, dst) in enumerate(
            ((left_in, left), (right_in, right), (left_t_in, left_t), (right_t_in, right_t), (kept, keptb)))
    ]

    def start_part(c, carry):
        for copy in load_part(c):
            copy.start()
        return carry

    def start_rest(c, carry):
        load_mom(c).start()
        load_weight(c).start()
        return carry

    start_part(0, 0)
    for copy in consts:
        copy.start()
    lax.fori_loop(1, CHUNKS, start_part, 0)
    lax.fori_loop(0, CHUNKS, start_rest, 0)

    barrier = pltpu.get_barrier_semaphore()
    pl.semaphore_signal(barrier, inc=1, device_id=sibling, device_id_type=MESH)

    def greet(k, carry):
        pl.semaphore_signal(barrier, inc=1, device_id=in_plane(k)[2], device_id_type=MESH)
        return carry

    lax.fori_loop(1, 16, greet, 0)
    for dz in (1, 2, 3):
        pl.semaphore_signal(barrier, inc=1, device_id=along_z(dz), device_id_type=MESH)
    pl.semaphore_wait(barrier, 19)

    def forward(block):
        lefted = split_dot((left[0], left[1]), block)
        return split_dot(lefted, (right[0], right[1]))

    def inverse(low):
        wide = split_dot(low, (right_t[0], right_t[1]))
        return split_dot((left_t[0], left_t[1]), wide)

    def sib_copy(c, n):
        return pltpu.make_async_remote_copy(
            src_ref=stage.at[c % SLOTS, n], dst_ref=sib.at[n, c],
            send_sem=ss_sem.at[c % SLOTS, n], recv_sem=sr_sem.at[c, n],
            device_id=sibling, device_id_type=MESH)

    def z_copy(c):
        return pltpu.make_async_remote_copy(
            src_ref=sib.at[0, c], dst_ref=zrecv.at[c],
            send_sem=zs_sem.at[c], recv_sem=zr_sem.at[c],
            device_id=partner, device_id_type=MESH)

    def send_stage(c):
        pltpu.make_async_copy(pbuf.at[c], pbuf.at[c], p_sem.at[c]).wait()
        for n in (0, 1):
            @pl.when(c >= SLOTS)
            def _():
                sib_copy(c, n).wait_send()
            stage[c % SLOTS, n] = pbuf[c, n].astype(f32)
            sib_copy(c, n).start()

    def process(g, half):
        c = 2 * g + half
        sib_copy(c, 0).wait_recv()
        sib[0, c] = sib[0, c] + pbuf[c, 2].astype(f32)
        z_copy(c).start()
        for h in (0, 1):
            cf[g, 1, 2 * half + h] = forward(sib[0, c, :, 256 * h:256 * h + 256])
        sib_copy(c, 1).wait_recv()
        load_mom(c).wait()
        sib[1, c] = sib[1, c] + pbuf[c, 3].astype(f32) + decay_rate * mombuf[c]
        for h in (0, 1):
            cf[g, 0, 2 * half + h] = forward(sib[1, c, :, 256 * h:256 * h + 256])

    def rs_send(g):
        def one(k, carry):
            py, px, target = in_plane(k)
            pltpu.make_async_remote_copy(
                src_ref=cf.at[g, :, py, pl.ds(pl.multiple_of(px * PIECE, 8), PIECE)],
                dst_ref=rsr.at[g, k - 1],
                send_sem=rs_s.at[g], recv_sem=rs_r.at[g],
                device_id=target, device_id_type=MESH).start()
            return carry
        lax.fori_loop(1, 16, one, 0)

    send_stage(0)
    for copy in consts:
        copy.wait()

    def gather_chip(g, carry):
        send_stage(2 * g + 1)
        process(g, 0)

        @pl.when(g < GROUPS - 1)
        def _():
            send_stage(2 * g + 2)
        process(g, 1)
        rs_send(g)
        return carry

    lax.fori_loop(0, GROUPS, gather_chip, 0)

    def band_words(b, carry):
        at = jnp.transpose(keptb[b])
        row, word = at // 32, jnp.left_shift(jnp.ones_like(at), at % 32)
        for k in range(16):
            rowbits[b, pl.ds(k, 1), :] = jnp.sum(jnp.where(row == k, word, 0), axis=0, keepdims=True)
        return carry

    lax.fori_loop(0, 6, band_words, 0)

    def group_mask(g, carry):
        words = rowbits[...].reshape(LOW, 224)
        upper = (words // 256).astype(f32).astype(jnp.bfloat16)
        lower = (words % 256).astype(f32).astype(jnp.bfloat16)
        block = lax.broadcasted_iota(jnp.int32, (224, 128), 0)
        lane = lax.broadcasted_iota(jnp.int32, (224, 128), 1)
        bit = lax.broadcasted_iota(jnp.int32, (LOW, 128), 1) % 16
        for j in range(4):
            spread = (block == (g * 4 + j) * 8 + lane // 16).astype(f32).astype(jnp.bfloat16)
            high = jnp.dot(upper, spread, preferred_element_type=f32)
            low = jnp.dot(lower, spread, preferred_element_type=f32)
            word = (high * 256.0 + low).astype(jnp.int32)
            mask[g, j] = (jnp.right_shift(word, bit) & 1).astype(f32)
        return carry

    lax.fori_loop(0, GROUPS, group_mask, 0)

    mine = pl.ds(pl.multiple_of(x * PIECE, 8), PIECE)

    def z3_copy(g, dz):
        return pltpu.make_async_remote_copy(
            src_ref=red.at[g, dz % 2], dst_ref=z3r.at[g, dz - 1],
            send_sem=z3_s.at[g, dz - 1], recv_sem=z3_r.at[g, dz - 1],
            device_id=along_z(dz), device_id_type=MESH)

    def sum_plane(g, carry):
        pltpu.make_async_copy(rsr.at[g], rsr.at[g], rs_r.at[g]).wait()
        for n in (0, 1):
            total = cf[g, n, y, mine]
            for k in range(15):
                total = total + rsr[g, k, n]
            red[g, n] = total
        for dz in (1, 2, 3):
            z3_copy(g, dz).start()
        return carry

    lax.fori_loop(0, GROUPS, sum_plane, 0)

    def sum_z(g, carry):
        for dz in (1, 2, 3):
            z3_copy(g, dz).wait_recv()
        mean[g, y, mine] = red[g, 0] + (z3r[g, 0] + z3r[g, 1] + z3r[g, 2])

        def one(k, inner):
            target = in_plane(k)[2]
            pltpu.make_async_remote_copy(
                src_ref=mean.at[g, y, mine], dst_ref=mean.at[g, y, mine],
                send_sem=ag_s.at[g], recv_sem=ag_r.at[g],
                device_id=target, device_id_type=MESH).start()
            return inner
        lax.fori_loop(1, 16, one, 0)
        return carry

    lax.fori_loop(0, GROUPS, sum_z, 0)

    def agg_copy(c):
        return pltpu.make_async_copy(mombuf.at[c], agg_out.at[:, columns(c)], oa_sem.at[c])

    def new_weight_copy(c):
        return pltpu.make_async_copy(wbuf.at[c], weight_out.at[:, columns(c)], ow_sem.at[c])

    def expand_mean(g, carry):
        pltpu.make_async_copy(rsr.at[g, :, 0], rsr.at[g, :, 0], ag_r.at[g]).wait()
        for half in (0, 1):
            c = 2 * g + half
            load_weight(c).wait()
            for h in (0, 1):
                j = 2 * half + h
                wide = slice(256 * h, 256 * h + 256)
                agg = inverse(mask[g, j] * (mean[g, j] / 32.0))
                mombuf[c, :, wide] = agg
                wbuf[c, :, wide] = (wbuf[c, :, wide].astype(f32) - step_rate * agg).astype(jnp.bfloat16)
            agg_copy(c).start()
            new_weight_copy(c).start()
        return carry

    lax.fori_loop(0, GROUPS, expand_mean, 0)

    def moment_copy(c):
        return pltpu.make_async_copy(zrecv.at[c], moment_out.at[0, :, columns(c)], om_sem.at[c])

    def finish(g, carry):
        for half in (0, 1):
            c = 2 * g + half
            z_copy(c).wait_recv()
            for h in (0, 1):
                wide = slice(256 * h, 256 * h + 256)
                moment = sib[1, c, :, wide] + zrecv[c, :, wide]
                zrecv[c, :, wide] = moment - inverse(mask[g, 2 * half + h] * forward(moment))
            moment_copy(c).start()
        return carry

    lax.fori_loop(0, GROUPS, finish, 0)

    for c in range(CHUNKS - SLOTS, CHUNKS):
        for n in (0, 1):
            sib_copy(c, n).wait_send()

    def drain_chunk(c, carry):
        z_copy(c).wait_send()
        agg_copy(c).wait()
        new_weight_copy(c).wait()
        moment_copy(c).wait()
        return carry

    def drain_group(g, carry):
        pltpu.make_async_copy(rsr.at[g], rsr.at[g], rs_s.at[g]).wait()
        pltpu.make_async_copy(rsr.at[g, :, 0], rsr.at[g, :, 0], ag_s.at[g]).wait()
        for dz in (1, 2, 3):
            z3_copy(g, dz).wait_send()
        return carry

    lax.fori_loop(0, GROUPS, drain_group, 0)
    lax.fori_loop(0, CHUNKS, drain_chunk, 0)


def per_device(partials, momentum, weight, kept):
    left, right, left_t, right_t = (jnp.asarray(t) for t in low_tables())
    f32, bf16, i32 = jnp.float32, jnp.bfloat16, jnp.int32
    dma = pltpu.SemaphoreType.DMA
    vmem = pltpu.VMEM
    hbm = pl.BlockSpec(memory_space=pl.ANY)
    return pl.pallas_call(
        kernel,
        out_shape=(
            jax.ShapeDtypeStruct((1, ROWS, QUARTER), f32),
            jax.ShapeDtypeStruct((ROWS, QUARTER), f32),
            jax.ShapeDtypeStruct((ROWS, QUARTER), bf16),
        ),
        in_specs=[hbm] * 8,
        out_specs=(hbm,) * 3,
        scratch_shapes=[
            vmem((CHUNKS, 4, ROWS, CHUNK), bf16),
            vmem((SLOTS, 2, ROWS, CHUNK), f32),
            vmem((2, CHUNKS, ROWS, CHUNK), f32),
            vmem((CHUNKS, ROWS, CHUNK), f32),
            vmem((CHUNKS, ROWS, CHUNK), f32),
            vmem((CHUNKS, ROWS, CHUNK), bf16),
            vmem((GROUPS, 2, 4, LOW, 128), f32),
            vmem((GROUPS, 15, 2, PIECE, 128), f32),
            vmem((GROUPS, 2, PIECE, 128), f32),
            vmem((GROUPS, 3, PIECE, 128), f32),
            vmem((GROUPS, 4, LOW, 128), f32),
            vmem((GROUPS, 4, LOW, 128), f32),
            vmem((6, 224, 64), i32),
            vmem((6, 16, 224), i32),
            vmem((2, LOW, ROWS), bf16),
            vmem((2, 256, 128), bf16),
            vmem((2, ROWS, LOW), bf16),
            vmem((2, 128, 256), bf16),
            dma((5,)), dma((CHUNKS,)), dma((CHUNKS,)), dma((CHUNKS,)),
            dma((SLOTS, 2)), dma((CHUNKS, 2)), dma((CHUNKS,)), dma((CHUNKS,)),
            dma((GROUPS,)), dma((GROUPS,)), dma((GROUPS, 3)), dma((GROUPS, 3)), dma((GROUPS,)), dma((GROUPS,)),
            dma((CHUNKS,)), dma((CHUNKS,)), dma((CHUNKS,)),
        ],
        compiler_params=pltpu.CompilerParams(
            collective_id=0, has_side_effects=True, vmem_limit_bytes=56 * 2 ** 20),
        cost_estimate=pl.CostEstimate(flops=8 * 10 ** 9, bytes_accessed=34 * 10 ** 6, transcendentals=0),
        name="compress_step",
    )(partials, momentum, weight, kept, left, right, left_t, right_t)


def solution(mesh):
    placed = (
        P("rep", "shard", None, None),
        P("rep", None, "shard"),
        P(None, "shard"),
        P(None, "shard", None),
    )
    return jax.shard_map(
        per_device,
        mesh=mesh,
        in_specs=placed,
        out_specs=(P("rep", None, "shard"), P(None, "shard"), P(None, "shard")),
        check_vma=False,
    )
```

time: 786 us -> 186 us (0.24)
  waiting for transfers between devices: 532 us -> 0 us
  Pallas kernels: 0 us -> 171 us
  matrix products: 115 us -> 0 us
  local copies, waits for them, and re-layouts: 89.4 us -> 13.1 us
  other arithmetic: 28.8 us -> 0 us
  between operations: 14.7 us -> 0.65 us
    psum x1 -> x0, waiting for transfers between devices: 346 us -> none  [per_device(): summed = lax.psum(sent, 'rep')]
    reduce_scatter x1 -> x0, waiting for transfers between devices: 186 us -> none  [per_device(): lax.psum_scatter(partial_rows, 'shard', scatter_dimension=1, tiled=True)]
    pallas_call x0 -> x1, Pallas kernels: none -> 171 us  [per_device(): pl.pallas_call(kernel, out_shape=(jax.ShapeDtypeStruct((1, ROWS, QUARTER)...]
    dot_general x16 -> x0, matrix products: 115 us -> none  [the longest x6 48.6 us: compress(): jnp.einsum('cjq,cq->cj', selector(kept_part[band_index]), corners[band_in...]
    reshape x10 -> x0, local copies, waits for them, and re-layouts: 31.8 us -> none  [the longest x1 13.2 us: expand_both(): corners.reshape(-1, 128)]
    slice x8 -> x0, local copies, waits for them, and re-layouts: 26.7 us -> none  [the longest x7 18.8 us: compress(): corners[band_index]]
    transpose x7 -> x0, local copies, waits for them, and re-layouts: 16.6 us -> none  [the longest x1 10.5 us: expand_both(): jnp.stack(placed, axis=1).reshape(pairs, count, blocks, 16, 16)]
    convert_element_type x3 -> x0, other arithmetic: 14.6 us -> none  [the longest x1 12.1 us: per_device(): partials.reshape(partials.shape[2], partials.shape[3]).astype(jnp.float32)]
  transfers between devices with their start and end apart: 2 -> 0, of which waited for: 2 -> 0; matrix products, arithmetic and copies ran while one was open for 1% -> 0% of each run, Pallas kernels for 0% -> 0%
where the time goes in v1:
time: 186 us; the launch traced here: 185 us
  Pallas kernels  171 us (92%)
  local copies, waits for them, and re-layouts  13.1 us (7%)
    pallas_call x1, Pallas kernels, per_device(): pl.pallas_call(kernel, out_shape=(jax.ShapeDtypeStruct((1, ROWS, QUARTER)...  171 us
    unnamed x8, local copies, waits for them, and re-layouts  13.1 us

profile of v1, /device:TPU:0, one launch (start us, length us, event | category | flops | bytes accessed | tf_op | source)
XLA Modules:
  0.0 184.7 jit_solution(322830980153094826)
XLA Ops:
  0.6 2.1 %copy.11.kept = s32[6,224,64]{2,1,0:T(8,128)} copy(s32[6,224,64]{1,2,0:T(8,128)} %param.11) | data formatting | bytes 688128 | tf_op args[3]
  2.7 170.9 %compress_step.1 = (f32[1,192,7168]{2,1,0:T(8,128)}, f32[192,7168]{1,0:T(8,128)}, bf16[192,7168]{1,0:T(8,128)(2,1)}) custom-call(bf16[1,1,192,28672]{3,2,1,0:T(8,128)(2,1)} %part.1, f32[1,192,7168]{2,1,0:T(8,128)} %mom.1, bf16[192,7168]{1,0:T(8,128)(2,1)} %wt.1, s32[6,224,64]{2,1,0:T(8,128)} %copy.11.kept, bf16[2,96,192]{2,1,0:T(8,128)(2,1)} %constant.8.clone.left_in, ...), custom_call_target="tpu_custom_call" | custom-call | flops 8000000000 | bytes 34000000 | tf_op jit(solution)/shard_map/compress_step/pallas_call | solution.py:332
  173.7 0.0 copy-start
  173.7 5.7 %copy.15 = f32[1,192,7168]{2,1,0:T(8,128)} copy(f32[1,192,7168]{2,1,0:T(8,128)} %get-tuple-element.6) | data formatting | bytes 11010048
  179.3 0.0 copy-done
  179.3 0.0 copy-start.1
  179.4 2.8 %copy.16 = f32[192,7168]{1,0:T(8,128)} copy(f32[192,7168]{1,0:T(8,128)S(1)} %copy-done) | data formatting | bytes 11010048
  182.2 1.0 copy-done.1
  183.1 1.5 copy.17
Async XLA Ops:
  173.7 5.7 %copy-start = (f32[192,7168]{1,0:T(8,128)S(1)}, f32[192,7168]{1,0:T(8,128)}, u32[]{:S(2)}) copy-start(f32[192,7168]{1,0:T(8,128)} %get-tuple-element.7) | copy-start | bytes 16515076
  179.3 3.8 %copy-start.1 = (bf16[192,7168]{1,0:T(8,128)(2,1)S(1)}, bf16[192,7168]{1,0:T(8,128)(2,1)}, u32[]{:S(2)}) copy-start(bf16[192,7168]{1,0:T(8,128)(2,1)} %get-tuple-element.8) | copy-start | bytes 8257540

commit v2 on v1

--- a/solution.py
+++ b/solution.py
@@ -20,6 +20,7 @@
 QUARTER = CHUNK * CHUNKS
 SLOTS = 4
 PIECE = 24
+EARLY = 7
 
 
 def low_tables():
@@ -30,13 +31,7 @@
     left = np.kron(np.eye(6), low)
     right = np.kron(np.eye(8), low.T)
 
-    def split(table):
-        table = table.astype(np.float32)
-        high = table.astype(jnp.bfloat16)
-        rest = (table - high.astype(np.float32)).astype(jnp.bfloat16)
-        return np.stack([high, rest])
-
-    return split(left), split(right), split(left.T.copy()), split(right.T.copy())
+    return tuple(np.ascontiguousarray(t, dtype=np.float32) for t in (left, right, left.T, right.T))
 
 
 def split_dot(a, b):
@@ -55,7 +50,7 @@
 def kernel(part, mom, wt, kept, left_in, right_in, left_t_in, right_t_in,
            moment_out, agg_out, weight_out,
            pbuf, stage, sib, zrecv, mombuf, wbuf, cf, rsr, red, z3r, mean, mask, keptb, rowbits,
-           left, right, left_t, right_t,
+           left32, right32, left_t32, right_t32, left, right, left_t, right_t,
            const_sem, p_sem, m_sem, w_sem, ss_sem, sr_sem, zs_sem, zr_sem,
            rs_s, rs_r, z3_s, z3_r, ag_s, ag_r, om_sem, oa_sem, ow_sem):
     f32 = jnp.float32
@@ -97,7 +92,7 @@
     consts = [
         pltpu.make_async_copy(src, dst, const_sem.at[n])
         for n, (src, dst) in enumerate(
-            ((left_in, left), (right_in, right), (left_t_in, left_t), (right_t_in, right_t), (kept, keptb)))
+            ((left_in, left32), (right_in, right32), (left_t_in, left_t32), (right_t_in, right_t32), (kept, keptb)))
     ]
 
     def start_part(c, carry):
@@ -161,7 +156,7 @@
         c = 2 * g + half
         sib_copy(c, 0).wait_recv()
         sib[0, c] = sib[0, c] + pbuf[c, 2].astype(f32)
-        z_copy(c).start()
+        pl.when(c < EARLY)(lambda: z_copy(c).start())
         for h in (0, 1):
             cf[g, 1, 2 * half + h] = forward(sib[0, c, :, 256 * h:256 * h + 256])
         sib_copy(c, 1).wait_recv()
@@ -184,6 +179,10 @@
     send_stage(0)
     for copy in consts:
         copy.wait()
+    for whole, pair in ((left32, left), (right32, right), (left_t32, left_t), (right_t32, right_t)):
+        high = whole[...].astype(jnp.bfloat16)
+        pair[0] = high
+        pair[1] = (whole[...] - high.astype(f32)).astype(jnp.bfloat16)
 
     def gather_chip(g, carry):
         send_stage(2 * g + 1)
@@ -199,7 +198,7 @@
     lax.fori_loop(0, GROUPS, gather_chip, 0)
 
     def band_words(b, carry):
-        at = jnp.transpose(keptb[b])
+        at = keptb[b]
         row, word = at // 32, jnp.left_shift(jnp.ones_like(at), at % 32)
         for k in range(16):
             rowbits[b, pl.ds(k, 1), :] = jnp.sum(jnp.where(row == k, word, 0), axis=0, keepdims=True)
@@ -244,6 +243,12 @@
         return carry
 
     lax.fori_loop(0, GROUPS, sum_plane, 0)
+
+    def start_z(c, carry):
+        z_copy(c).start()
+        return carry
+
+    lax.fori_loop(EARLY, CHUNKS, start_z, 0)
 
     def sum_z(g, carry):
         for dz in (1, 2, 3):
@@ -351,8 +356,12 @@
             vmem((GROUPS, 3, PIECE, 128), f32),
             vmem((GROUPS, 4, LOW, 128), f32),
             vmem((GROUPS, 4, LOW, 128), f32),
-            vmem((6, 224, 64), i32),
+            vmem((6, 64, 224), i32),
             vmem((6, 16, 224), i32),
+            vmem((LOW, ROWS), f32),
+            vmem((256, 128), f32),
+            vmem((ROWS, LOW), f32),
+            vmem((128, 256), f32),
             vmem((2, LOW, ROWS), bf16),
             vmem((2, 256, 128), bf16),
             vmem((2, ROWS, LOW), bf16),
@@ -366,7 +375,7 @@
             collective_id=0, has_side_effects=True, vmem_limit_bytes=56 * 2 ** 20),
         cost_estimate=pl.CostEstimate(flops=8 * 10 ** 9, bytes_accessed=34 * 10 ** 6, transcendentals=0),
         name="compress_step",
-    )(partials, momentum, weight, kept, left, right, left_t, right_t)
+    )(partials, momentum, weight, jnp.transpose(kept, (0, 2, 1)), left, right, left_t, right_t)
 
 
 def solution(mesh):

time: 186 us -> 149 us (0.80)
  Pallas kernels: 171 us -> 136 us
  local copies, waits for them, and re-layouts: 13.1 us -> 11 us
    pallas_call x1, Pallas kernels: 171 us -> 136 us  [per_device(): pl.pallas_call(kernel, out_shape=(jax.ShapeDtypeStruct((1, ROWS, QUARTER)...]
    unnamed x8 -> x7, local copies, waits for them, and re-layouts: 13.1 us -> 11 us
where the time goes in v2:
time: 149 us; the launch traced here: 148 us
  Pallas kernels  136 us (91%)
  local copies, waits for them, and re-layouts  11 us (7%)
    pallas_call x1, Pallas kernels, per_device(): pl.pallas_call(kernel, out_shape=(jax.ShapeDtypeStruct((1, ROWS, QUARTER)...  136 us
    unnamed x7, local copies, waits for them, and re-layouts  11 us

profile of v2, /device:TPU:0, one launch (start us, length us, event | category | flops | bytes accessed | tf_op | source)
XLA Modules:
  0.0 147.8 jit_solution(12287175157827157475)
XLA Ops:
  0.6 136.2 %compress_step.1 = (f32[1,192,7168]{2,1,0:T(8,128)}, f32[192,7168]{1,0:T(8,128)}, bf16[192,7168]{1,0:T(8,128)(2,1)}) custom-call(bf16[1,1,192,28672]{3,2,1,0:T(8,128)(2,1)} %part.1, f32[1,192,7168]{2,1,0:T(8,128)} %mom.1, bf16[192,7168]{1,0:T(8,128)(2,1)} %wt.1, s32[6,64,224]{2,1,0:T(8,128)} %bitcast.1, f32[96,192]{1,0:T(8,128)} %constant.8.clone.left_in, ...), custom_call_target="tpu_custom_call" | custom-call | flops 8000000000 | bytes 34000000 | tf_op jit(solution)/shard_map/compress_step/pallas_call | solution.py:337
  136.8 0.0 copy-start
  136.8 5.7 %copy.14 = f32[1,192,7168]{2,1,0:T(8,128)} copy(f32[1,192,7168]{2,1,0:T(8,128)} %get-tuple-element.6) | data formatting | bytes 11010048
  142.5 0.0 copy-done
  142.5 0.0 copy-start.1
  142.5 2.8 %copy.15 = f32[192,7168]{1,0:T(8,128)} copy(f32[192,7168]{1,0:T(8,128)S(1)} %copy-done) | data formatting | bytes 11010048
  145.3 1.0 copy-done.1
  146.3 1.5 %copy.16 = bf16[192,7168]{1,0:T(8,128)(2,1)} copy(bf16[192,7168]{1,0:T(8,128)(2,1)S(1)} %copy-done.1) | data formatting | bytes 5505024
Async XLA Ops:
  136.8 5.7 %copy-start = (f32[192,7168]{1,0:T(8,128)S(1)}, f32[192,7168]{1,0:T(8,128)}, u32[]{:S(2)}) copy-start(f32[192,7168]{1,0:T(8,128)} %get-tuple-element.7) | copy-start | bytes 16515076
  142.5 3.8 %copy-start.1 = (bf16[192,7168]{1,0:T(8,128)(2,1)S(1)}, bf16[192,7168]{1,0:T(8,128)(2,1)}, u32[]{:S(2)}) copy-start(bf16[192,7168]{1,0:T(8,128)(2,1)} %get-tuple-element.8) | copy-start | bytes 8257540

commit v3 on v2

--- a/solution.py
+++ b/solution.py
@@ -19,6 +19,7 @@
 GROUPS = 7
 QUARTER = CHUNK * CHUNKS
 SLOTS = 4
+LOADS = 8
 PIECE = 24
 EARLY = 7
 
@@ -52,7 +53,7 @@
            pbuf, stage, sib, zrecv, mombuf, wbuf, cf, rsr, red, z3r, mean, mask, keptb, rowbits,
            left32, right32, left_t32, right_t32, left, right, left_t, right_t,
            const_sem, p_sem, m_sem, w_sem, ss_sem, sr_sem, zs_sem, zr_sem,
-           rs_s, rs_r, z3_s, z3_r, ag_s, ag_r, om_sem, oa_sem, ow_sem):
+           rs_s, rs_r, z3_s, z3_r, ag_s, ag_r, om_sem, oa_sem, ow_sem, ready_sem, plane_sem):
     f32 = jnp.float32
     rep, shard = lax.axis_index("rep"), lax.axis_index("shard")
     plane, z_hi = rep // 2, rep % 2
@@ -76,7 +77,7 @@
         return [
             pltpu.make_async_copy(
                 part.at[0, 0, :, pl.ds(pl.multiple_of(q * QUARTER + c * CHUNK, CHUNK), CHUNK)],
-                pbuf.at[c, n], p_sem.at[c])
+                pbuf.at[c % LOADS, n], p_sem.at[c % LOADS])
             for n, q in enumerate(quarters)
         ]
 
@@ -105,23 +106,42 @@
         load_weight(c).start()
         return carry
 
+    barrier = pltpu.get_barrier_semaphore()
+    leads = z_lo == core
+
+    @pl.when(jnp.logical_not(leads))
+    def _():
+        for other in (sibling, partner):
+            pl.semaphore_signal(barrier, inc=1, device_id=other, device_id_type=MESH)
+
     start_part(0, 0)
-    for copy in consts:
-        copy.start()
-    lax.fori_loop(1, CHUNKS, start_part, 0)
-    lax.fori_loop(0, CHUNKS, start_rest, 0)
-
-    barrier = pltpu.get_barrier_semaphore()
-    pl.semaphore_signal(barrier, inc=1, device_id=sibling, device_id_type=MESH)
-
-    def greet(k, carry):
-        pl.semaphore_signal(barrier, inc=1, device_id=in_plane(k)[2], device_id_type=MESH)
-        return carry
-
-    lax.fori_loop(1, 16, greet, 0)
-    for dz in (1, 2, 3):
-        pl.semaphore_signal(barrier, inc=1, device_id=along_z(dz), device_id_type=MESH)
-    pl.semaphore_wait(barrier, 19)
+
+    @pl.when(leads)
+    def _():
+        pl.semaphore_wait(barrier, 2)
+        for other in (sibling, partner):
+            pl.semaphore_signal(ready_sem, inc=1, device_id=other, device_id_type=MESH)
+
+    @pl.when(jnp.logical_not(leads))
+    def _():
+        pl.semaphore_wait(ready_sem, 2)
+
+        def greet(k, carry):
+            pl.semaphore_signal(barrier, inc=1, device_id=in_plane(k)[2], device_id_type=MESH)
+            return carry
+
+        lax.fori_loop(1, 16, greet, 0)
+        pl.semaphore_signal(barrier, inc=1, device_id=along_z(2), device_id_type=MESH)
+
+    def meet_plane():
+        @pl.when(jnp.logical_not(leads))
+        def _():
+            pl.semaphore_wait(barrier, 16)
+            pl.semaphore_signal(plane_sem, inc=1, device_id=sibling, device_id_type=MESH)
+
+        @pl.when(leads)
+        def _():
+            pl.semaphore_wait(plane_sem, 1)
 
     def forward(block):
         lefted = split_dot((left[0], left[1]), block)
@@ -144,24 +164,25 @@
             device_id=partner, device_id_type=MESH)
 
     def send_stage(c):
-        pltpu.make_async_copy(pbuf.at[c], pbuf.at[c], p_sem.at[c]).wait()
+        pltpu.make_async_copy(pbuf.at[c % LOADS], pbuf.at[c % LOADS], p_sem.at[c % LOADS]).wait()
         for n in (0, 1):
             @pl.when(c >= SLOTS)
             def _():
                 sib_copy(c, n).wait_send()
-            stage[c % SLOTS, n] = pbuf[c, n].astype(f32)
+            stage[c % SLOTS, n] = pbuf[c % LOADS, n].astype(f32)
             sib_copy(c, n).start()
 
     def process(g, half):
         c = 2 * g + half
         sib_copy(c, 0).wait_recv()
-        sib[0, c] = sib[0, c] + pbuf[c, 2].astype(f32)
+        sib[0, c] = sib[0, c] + pbuf[c % LOADS, 2].astype(f32)
         pl.when(c < EARLY)(lambda: z_copy(c).start())
         for h in (0, 1):
             cf[g, 1, 2 * half + h] = forward(sib[0, c, :, 256 * h:256 * h + 256])
         sib_copy(c, 1).wait_recv()
         load_mom(c).wait()
-        sib[1, c] = sib[1, c] + pbuf[c, 3].astype(f32) + decay_rate * mombuf[c]
+        sib[1, c] = sib[1, c] + pbuf[c % LOADS, 3].astype(f32) + decay_rate * mombuf[c]
+        pl.when(c + LOADS < CHUNKS)(lambda: start_part(c + LOADS, None))
         for h in (0, 1):
             cf[g, 0, 2 * half + h] = forward(sib[1, c, :, 256 * h:256 * h + 256])
 
@@ -178,6 +199,10 @@
 
     send_stage(0)
     for copy in consts:
+        copy.start()
+    lax.fori_loop(1, LOADS, start_part, 0)
+    lax.fori_loop(0, CHUNKS, start_rest, 0)
+    for copy in consts:
         copy.wait()
     for whole, pair in ((left32, left), (right32, right), (left_t32, left_t), (right_t32, right_t)):
         high = whole[...].astype(jnp.bfloat16)
@@ -192,6 +217,7 @@
         def _():
             send_stage(2 * g + 2)
         process(g, 1)
+        pl.when(g == 0)(meet_plane)
         rs_send(g)
         return carry
 
@@ -225,11 +251,12 @@
 
     mine = pl.ds(pl.multiple_of(x * PIECE, 8), PIECE)
 
-    def z3_copy(g, dz):
+    def z3_copy(g, step):
+        target = along_z(jnp.where(z_lo == 1, 1, 3)) if step == 0 else along_z(2)
         return pltpu.make_async_remote_copy(
-            src_ref=red.at[g, dz % 2], dst_ref=z3r.at[g, dz - 1],
-            send_sem=z3_s.at[g, dz - 1], recv_sem=z3_r.at[g, dz - 1],
-            device_id=along_z(dz), device_id_type=MESH)
+            src_ref=red.at[g, 1 - step], dst_ref=z3r.at[g, step],
+            send_sem=z3_s.at[g, step], recv_sem=z3_r.at[g, step],
+            device_id=target, device_id_type=MESH)
 
     def sum_plane(g, carry):
         pltpu.make_async_copy(rsr.at[g], rsr.at[g], rs_r.at[g]).wait()
@@ -238,11 +265,18 @@
             for k in range(15):
                 total = total + rsr[g, k, n]
             red[g, n] = total
-        for dz in (1, 2, 3):
-            z3_copy(g, dz).start()
+        z3_copy(g, 0).start()
         return carry
 
     lax.fori_loop(0, GROUPS, sum_plane, 0)
+
+    def sum_pair(g, carry):
+        z3_copy(g, 0).wait_recv()
+        red[g, 0] = red[g, 0] + z3r[g, 0]
+        z3_copy(g, 1).start()
+        return carry
+
+    lax.fori_loop(0, GROUPS, sum_pair, 0)
 
     def start_z(c, carry):
         z_copy(c).start()
@@ -251,9 +285,8 @@
     lax.fori_loop(EARLY, CHUNKS, start_z, 0)
 
     def sum_z(g, carry):
-        for dz in (1, 2, 3):
-            z3_copy(g, dz).wait_recv()
-        mean[g, y, mine] = red[g, 0] + (z3r[g, 0] + z3r[g, 1] + z3r[g, 2])
+        z3_copy(g, 1).wait_recv()
+        mean[g, y, mine] = red[g, 0] + z3r[g, 1]
 
         def one(k, inner):
             target = in_plane(k)[2]
@@ -320,12 +353,27 @@
     def drain_group(g, carry):
         pltpu.make_async_copy(rsr.at[g], rsr.at[g], rs_s.at[g]).wait()
         pltpu.make_async_copy(rsr.at[g, :, 0], rsr.at[g, :, 0], ag_s.at[g]).wait()
-        for dz in (1, 2, 3):
-            z3_copy(g, dz).wait_send()
+        for step in (0, 1):
+            z3_copy(g, step).wait_send()
         return carry
 
     lax.fori_loop(0, GROUPS, drain_group, 0)
     lax.fori_loop(0, CHUNKS, drain_chunk, 0)
+
+
+def write_out(*refs):
+    ins, outs, sem = refs[:3], refs[3:6], refs[6]
+    copies = []
+    for n, (src, dst) in enumerate(zip(ins, outs)):
+        if n == 0:
+            src, dst = src.at[0], dst.at[0]
+        for b in range(6):
+            rows = pl.ds(32 * b, 32)
+            copies.append(pltpu.make_async_copy(src.at[rows], dst.at[rows], sem.at[b, n]))
+    for copy in copies:
+        copy.start()
+    for copy in copies:
+        copy.wait()
 
 
 def per_device(partials, momentum, weight, kept):
@@ -334,17 +382,17 @@
     dma = pltpu.SemaphoreType.DMA
     vmem = pltpu.VMEM
     hbm = pl.BlockSpec(memory_space=pl.ANY)
-    return pl.pallas_call(
+    results = pl.pallas_call(
         kernel,
         out_shape=(
-            jax.ShapeDtypeStruct((1, ROWS, QUARTER), f32),
-            jax.ShapeDtypeStruct((ROWS, QUARTER), f32),
-            jax.ShapeDtypeStruct((ROWS, QUARTER), bf16),
+            vmem((1, ROWS, QUARTER), f32),
+            vmem((ROWS, QUARTER), f32),
+            vmem((ROWS, QUARTER), bf16),
         ),
         in_specs=[hbm] * 8,
         out_specs=(hbm,) * 3,
         scratch_shapes=[
-            vmem((CHUNKS, 4, ROWS, CHUNK), bf16),
+            vmem((LOADS, 4, ROWS, CHUNK), bf16),
             vmem((SLOTS, 2, ROWS, CHUNK), f32),
             vmem((2, CHUNKS, ROWS, CHUNK), f32),
             vmem((CHUNKS, ROWS, CHUNK), f32),
@@ -353,7 +401,7 @@
             vmem((GROUPS, 2, 4, LOW, 128), f32),
             vmem((GROUPS, 15, 2, PIECE, 128), f32),
             vmem((GROUPS, 2, PIECE, 128), f32),
-            vmem((GROUPS, 3, PIECE, 128), f32),
+            vmem((GROUPS, 2, PIECE, 128), f32),
             vmem((GROUPS, 4, LOW, 128), f32),
             vmem((GROUPS, 4, LOW, 128), f32),
             vmem((6, 64, 224), i32),
@@ -366,16 +414,26 @@
             vmem((2, 256, 128), bf16),
             vmem((2, ROWS, LOW), bf16),
             vmem((2, 128, 256), bf16),
-            dma((5,)), dma((CHUNKS,)), dma((CHUNKS,)), dma((CHUNKS,)),
+            dma((5,)), dma((LOADS,)), dma((CHUNKS,)), dma((CHUNKS,)),
             dma((SLOTS, 2)), dma((CHUNKS, 2)), dma((CHUNKS,)), dma((CHUNKS,)),
-            dma((GROUPS,)), dma((GROUPS,)), dma((GROUPS, 3)), dma((GROUPS, 3)), dma((GROUPS,)), dma((GROUPS,)),
+            dma((GROUPS,)), dma((GROUPS,)), dma((GROUPS, 2)), dma((GROUPS, 2)), dma((GROUPS,)), dma((GROUPS,)),
             dma((CHUNKS,)), dma((CHUNKS,)), dma((CHUNKS,)),
+            pltpu.SemaphoreType.REGULAR, pltpu.SemaphoreType.REGULAR,
         ],
         compiler_params=pltpu.CompilerParams(
-            collective_id=0, has_side_effects=True, vmem_limit_bytes=56 * 2 ** 20),
+            collective_id=0, has_side_effects=True, vmem_limit_bytes=46 * 2 ** 20),
         cost_estimate=pl.CostEstimate(flops=8 * 10 ** 9, bytes_accessed=34 * 10 ** 6, transcendentals=0),
         name="compress_step",
     )(partials, momentum, weight, jnp.transpose(kept, (0, 2, 1)), left, right, left_t, right_t)
+    return pl.pallas_call(
+        write_out,
+        out_shape=tuple(jax.ShapeDtypeStruct(r.shape, r.dtype) for r in results),
+        in_specs=[hbm] * 3,
+        out_specs=(hbm,) * 3,
+        scratch_shapes=[dma((6, 3))],
+        compiler_params=pltpu.CompilerParams(vmem_limit_bytes=2 ** 20),
+        name="write_out",
+    )(*(pltpu.with_memory_space_constraint(r, vmem) for r in results))
 
 
 def solution(mesh):

time: 149 us -> 136 us (0.913)
  local copies, waits for them, and re-layouts: 11 us -> 0 us
    unnamed x7 -> x0, local copies, waits for them, and re-layouts: 11 us -> none
    pallas_call x1 -> x2, Pallas kernels: 136 us -> 135 us  [the longest x1 130 us: per_device(): pl.pallas_call(kernel, out_shape=(vmem((1, ROWS, QUARTER), f32), vmem((RO...]
where the time goes in v3:
time: 136 us
  Pallas kernels  135 us (99%)
    pallas_call x1, Pallas kernels, per_device(): pl.pallas_call(kernel, out_shape=(vmem((1, ROWS, QUARTER), f32), vmem((RO...  130 us
    pallas_call x1, Pallas kernels, per_device(): pl.pallas_call(write_out, out_shape=tuple((jax.ShapeDtypeStruct(r.shape,...  5.06 us

profile of v3, /device:TPU:0, one launch (start us, length us, event | category | flops | bytes accessed | tf_op | source)
XLA Modules:
  0.0 135.7 jit_solution(5930603417643817932)
XLA Ops:
  0.6 130.0 %compress_step.1 = (f32[1,192,7168]{2,1,0:T(8,128)S(1)}, f32[192,7168]{1,0:T(8,128)S(1)}, bf16[192,7168]{1,0:T(8,128)(2,1)S(1)}) custom-call(bf16[1,1,192,28672]{3,2,1,0:T(8,128)(2,1)} %part.1, f32[1,192,7168]{2,1,0:T(8,128)} %mom.1, bf16[192,7168]{1,0:T(8,128)(2,1)} %wt.1, s32[6,64,224]{2,1,0:T(8,128)} %bitcast.1, f32[96,192]{1,0:T(8,128)} %constant.8.clone.left_in, ...), custom_call_target="tpu_custom_call" | custom-call | flops 8000000000 | bytes 34000000 | tf_op jit(solution)/shard_map/compress_step/pallas_call | solution.py:385
  130.6 5.1 %write_out.1 = (f32[1,192,7168]{2,1,0:T(8,128)}, f32[192,7168]{1,0:T(8,128)}, bf16[192,7168]{1,0:T(8,128)(2,1)}) custom-call(f32[1,192,7168]{2,1,0:T(8,128)S(1)} %get-tuple-element.6.refs_0_, f32[192,7168]{1,0:T(8,128)S(1)} %get-tuple-element.7.refs_1_, bf16[192,7168]{1,0:T(8,128)(2,1)S(1)} %get-tuple-element.8.refs_2_), custom_call_target="tpu_custom_call" | custom-call | tf_op jit(solution)/shard_map/write_out/pallas_call | solution.py:428

commit v4 on v3

--- a/solution.py
+++ b/solution.py
@@ -14,46 +14,57 @@
 MESH = pl.DeviceIdType.MESH
 ROWS = 192
 LOW = 96
-CHUNK = 512
-CHUNKS = 14
+CHUNK = 256
+CHUNKS = 28
 GROUPS = 7
 QUARTER = CHUNK * CHUNKS
-SLOTS = 4
-LOADS = 8
+SLOTS = 8
+LOADS = 16
 PIECE = 24
-EARLY = 7
-
-
-def low_tables():
-    freq = np.arange(16, dtype=np.float64)[:, None]
+MOVES = 4
+AHEAD = 3
+MIDDLE = 4
+RAW = 2
+HALF = 2 * ROWS
+PACKED = 360
+EARLY = 20
+
+
+def tables():
+    freq = np.arange(32, dtype=np.float64)[:, None]
     place = np.arange(32, dtype=np.float64)[None, :]
-    low = np.cos(np.pi * (2.0 * place + 1.0) * freq / 64.0) * np.sqrt(2.0 / 32.0)
-    low[0] *= np.sqrt(0.5)
-    left = np.kron(np.eye(6), low)
-    right = np.kron(np.eye(8), low.T)
-
+    dct = np.cos(np.pi * (2.0 * place + 1.0) * freq / 64.0) * np.sqrt(2.0 / 32.0)
+    dct[0] *= np.sqrt(0.5)
+    left = np.zeros((ROWS, ROWS))
+    for band in range(6):
+        for k in range(16):
+            left[32 * (band // 2) + 2 * k + band % 2, 32 * band:32 * band + 32] = dct[k]
+            left[LOW + 16 * band + k, 32 * band:32 * band + 32] = dct[16 + k]
+    right = np.concatenate([np.kron(np.eye(8), dct[:16].T), np.kron(np.eye(8), dct[16:].T)], axis=1)
     return tuple(np.ascontiguousarray(t, dtype=np.float32) for t in (left, right, left.T, right.T))
 
 
+def two_terms(v):
+    high = v.astype(jnp.bfloat16)
+    return high, (v - high.astype(jnp.float32)).astype(jnp.bfloat16)
+
+
 def split_dot(a, b):
-    if isinstance(a, tuple):
-        a_high, a_rest = a
-        b_high = b.astype(jnp.bfloat16)
-        b_rest = (b - b_high.astype(jnp.float32)).astype(jnp.bfloat16)
-    else:
-        b_high, b_rest = b
-        a_high = a.astype(jnp.bfloat16)
-        a_rest = (a - a_high.astype(jnp.float32)).astype(jnp.bfloat16)
+    a_high, a_rest = a if isinstance(a, tuple) else two_terms(a)
+    b_high, b_rest = b if isinstance(b, tuple) else two_terms(b)
+    rows = a_high.shape[0]
     dot = functools.partial(jnp.dot, preferred_element_type=jnp.float32)
-    return dot(a_high, b_high) + (dot(a_high, b_rest) + dot(a_rest, b_high))
+    first = dot(jnp.concatenate([a_high, a_rest], axis=0), b_high)
+    return first[:rows] + (first[rows:] + dot(a_high, b_rest))
 
 
 def kernel(part, mom, wt, kept, left_in, right_in, left_t_in, right_t_in,
            moment_out, agg_out, weight_out,
-           pbuf, stage, sib, zrecv, mombuf, wbuf, cf, rsr, red, z3r, mean, mask, keptb, rowbits,
+           pbuf, stage, stage_far, own, far, zrecv, mombuf, wbuf, cf, rsr, red, z3r, mean, mask, keptb, rowbits,
+           kept_far, words_far, gives_of, same, before, above,
            left32, right32, left_t32, right_t32, left, right, left_t, right_t,
            const_sem, p_sem, m_sem, w_sem, ss_sem, sr_sem, zs_sem, zr_sem,
-           rs_s, rs_r, z3_s, z3_r, ag_s, ag_r, om_sem, oa_sem, ow_sem, ready_sem, plane_sem):
+           rs_s, rs_r, z3_s, z3_r, ag_s, ag_r, om_sem, oa_sem, ow_sem, k_sem, ready_sem, plane_sem):
     f32 = jnp.float32
     rep, shard = lax.axis_index("rep"), lax.axis_index("shard")
     plane, z_hi = rep // 2, rep % 2
@@ -144,22 +155,94 @@
             pl.semaphore_wait(plane_sem, 1)
 
     def forward(block):
-        lefted = split_dot((left[0], left[1]), block)
-        return split_dot(lefted, (right[0], right[1]))
+        lefted = split_dot((left[0, :LOW], left[1, :LOW]), block)
+        return split_dot(lefted, (right[0, :, :128], right[1, :, :128]))
 
     def inverse(low):
-        wide = split_dot(low, (right_t[0], right_t[1]))
-        return split_dot((left_t[0], left_t[1]), wide)
+        wide = split_dot(low, (right_t[0, :128], right_t[1, :128]))
+        return split_dot((left_t[0, :, :LOW], left_t[1, :, :LOW]), wide)
+
+    row = lax.broadcasted_iota(jnp.int32, (LOW, 128), 0) % 32 // 2
+    lane = lax.broadcasted_iota(jnp.int32, (LOW, 128), 1) % 16
+
+    def turn(v, shift, axis):
+        return pltpu.roll(v, shift % v.shape[axis], axis)
+
+    def from_later(v, step):
+        if step >= 4:
+            return turn(v, -(2 << (step - 4)), 0)
+        far = 1 << step
+        return jnp.where(lane + far < 16, turn(v, -far, 1), turn(turn(v, -2, 0), 16 - far, 1))
+
+    def from_earlier(v, step):
+        if step >= 4:
+            return turn(v, 2 << (step - 4), 0)
+        far = 1 << step
+        return jnp.where(lane >= far, turn(v, far, 1), turn(turn(v, 2, 0), -(16 - far), 1))
+
+    def unpack_words(words, at):
+        def band_words(p, carry):
+            for b in (0, 1):
+                where = at[2 * p + b]
+                k_of, word = where // 32, jnp.left_shift(jnp.ones_like(where), where % 32)
+                for k in range(16):
+                    words[p, pl.ds(2 * k + b, 1), :] = jnp.sum(
+                        jnp.where(k_of == k, word, 0), axis=0, keepdims=True)
+            return carry
+
+        lax.fori_loop(0, 3, band_words, 0)
+
+    def kept_mask(words, c):
+        word = words[...].reshape(LOW, 224)
+        upper = (word // 256).astype(f32).astype(jnp.bfloat16)
+        lower = (word % 256).astype(f32).astype(jnp.bfloat16)
+        block = lax.broadcasted_iota(jnp.int32, (224, 128), 0)
+        block_of = c * 8 + lax.broadcasted_iota(jnp.int32, (224, 128), 1) // 16
+        spread = (block == block_of).astype(f32).astype(jnp.bfloat16)
+        high = jnp.dot(upper, spread, preferred_element_type=f32)
+        low = jnp.dot(lower, spread, preferred_element_type=f32)
+        return jnp.right_shift((high * 256.0 + low).astype(jnp.int32), lane) & 1
+
+    def moves(masks):
+        dot = functools.partial(jnp.dot, preferred_element_type=f32)
+        place = 16 * row + lane
+        to_go = []
+        for kept_here in masks:
+            flags = kept_here.astype(f32).astype(jnp.bfloat16)
+            in_rows = dot(flags, same[...]).astype(jnp.bfloat16)
+            count = dot(flags, before[...]) + dot(above[...], in_rows)
+            to_go.append(jnp.where(kept_here == 1, 0, count.astype(jnp.int32)))
+        taken = [jnp.zeros_like(m) for m in masks]
+        given = [jnp.zeros_like(m) for m in masks]
+        for step in range(7):
+            there = place + (1 << step) < 256
+            for n, now in enumerate(to_go):
+                coming = jnp.where(there, from_later(now, step), 0)
+                takes, gives = coming & (1 << step), now & (1 << step)
+                taken[n], given[n] = taken[n] | takes, given[n] | gives
+                to_go[n] = jnp.where(takes != 0, coming, jnp.where(gives != 0, 0, now))
+        return taken, given
+
+    def pack(lows, taken):
+        for step in range(7):
+            lows = [jnp.where(t & (1 << step) != 0, from_later(low, step), low) for low, t in zip(lows, taken)]
+        return lows
+
+    def unpack(lows, given):
+        for step in reversed(range(7)):
+            lows = [jnp.where(t & (1 << step) != 0, from_earlier(low, step), low) for low, t in zip(lows, given)]
+        return lows
 
     def sib_copy(c, n):
+        src, dst = ((stage_far, far), (stage, own))[n]
         return pltpu.make_async_remote_copy(
-            src_ref=stage.at[c % SLOTS, n], dst_ref=sib.at[n, c],
+            src_ref=src.at[c % SLOTS], dst_ref=dst.at[c],
             send_sem=ss_sem.at[c % SLOTS, n], recv_sem=sr_sem.at[c, n],
             device_id=sibling, device_id_type=MESH)
 
-    def z_copy(c):
+    def z_copy(c, rows):
         return pltpu.make_async_remote_copy(
-            src_ref=sib.at[0, c], dst_ref=zrecv.at[c],
+            src_ref=far.at[c, pl.ds(0, rows)], dst_ref=zrecv.at[c, pl.ds(0, rows)],
             send_sem=zs_sem.at[c], recv_sem=zr_sem.at[c],
             device_id=partner, device_id_type=MESH)
 
@@ -169,22 +252,45 @@
             @pl.when(c >= SLOTS)
             def _():
                 sib_copy(c, n).wait_send()
-            stage[c % SLOTS, n] = pbuf[c % LOADS, n].astype(f32)
+            value = pbuf[c % LOADS, n].astype(f32)
+            if n == 0:
+                stage_far[c % SLOTS, :ROWS] = value[:, :128]
+                stage_far[c % SLOTS, ROWS:] = value[:, 128:]
+            else:
+                stage[c % SLOTS] = value
             sib_copy(c, n).start()
 
-    def process(g, half):
-        c = 2 * g + half
+    def process(g, j, packed):
+        c = 4 * g + j
         sib_copy(c, 0).wait_recv()
-        sib[0, c] = sib[0, c] + pbuf[c % LOADS, 2].astype(f32)
-        pl.when(c < EARLY)(lambda: z_copy(c).start())
-        for h in (0, 1):
-            cf[g, 1, 2 * half + h] = forward(sib[0, c, :, 256 * h:256 * h + 256])
+        mine_far = pbuf[c % LOADS, 2].astype(f32)
+        chip = jnp.concatenate([far[c, :ROWS] + mine_far[:, :128], far[c, ROWS:] + mine_far[:, 128:]], axis=1)
+        if not packed:
+            far[c, :ROWS] = chip[:, :128]
+            far[c, ROWS:] = chip[:, 128:]
+            z_copy(c, HALF).start()
+            cf[g, 1, j] = forward(chip)
+        else:
+            lefted = split_dot((left[0], left[1]), chip)
+            righted = split_dot(lefted[:LOW], (right[0], right[1]))
+            cf[g, 1, j] = righted[:, :128]
+            far[c, :LOW] = lefted[LOW:, :128]
+            far[c, LOW:ROWS] = lefted[LOW:, 128:]
+            far[c, ROWS:ROWS + LOW] = righted[:, 128:]
         sib_copy(c, 1).wait_recv()
         load_mom(c).wait()
-        sib[1, c] = sib[1, c] + pbuf[c % LOADS, 3].astype(f32) + decay_rate * mombuf[c]
+        own[c] = own[c] + pbuf[c % LOADS, 3].astype(f32) + decay_rate * mombuf[c]
         pl.when(c + LOADS < CHUNKS)(lambda: start_part(c + LOADS, None))
-        for h in (0, 1):
-            cf[g, 0, 2 * half + h] = forward(sib[1, c, :, 256 * h:256 * h + 256])
+        cf[g, 0, j] = forward(own[c])
+
+    def pack_pair(g, j):
+        taken, _ = moves([kept_mask(words_far, 4 * g + j + n) for n in (0, 1)])
+        lows = pack([cf[g, 1, j + n] for n in (0, 1)], taken)
+        for n, low in enumerate(lows):
+            c = 4 * g + j + n
+            for p in range(3):
+                far[c, ROWS + LOW + 24 * p:ROWS + LOW + 24 * p + 24] = low[32 * p:32 * p + 24]
+            pl.when(c < EARLY)(lambda c=c: z_copy(c, PACKED).start())
 
     def rs_send(g):
         def one(k, carry):
@@ -209,45 +315,10 @@
         pair[0] = high
         pair[1] = (whole[...] - high.astype(f32)).astype(jnp.bfloat16)
 
-    def gather_chip(g, carry):
-        send_stage(2 * g + 1)
-        process(g, 0)
-
-        @pl.when(g < GROUPS - 1)
-        def _():
-            send_stage(2 * g + 2)
-        process(g, 1)
-        pl.when(g == 0)(meet_plane)
-        rs_send(g)
-        return carry
-
-    lax.fori_loop(0, GROUPS, gather_chip, 0)
-
-    def band_words(b, carry):
-        at = keptb[b]
-        row, word = at // 32, jnp.left_shift(jnp.ones_like(at), at % 32)
-        for k in range(16):
-            rowbits[b, pl.ds(k, 1), :] = jnp.sum(jnp.where(row == k, word, 0), axis=0, keepdims=True)
-        return carry
-
-    lax.fori_loop(0, 6, band_words, 0)
-
-    def group_mask(g, carry):
-        words = rowbits[...].reshape(LOW, 224)
-        upper = (words // 256).astype(f32).astype(jnp.bfloat16)
-        lower = (words % 256).astype(f32).astype(jnp.bfloat16)
-        block = lax.broadcasted_iota(jnp.int32, (224, 128), 0)
-        lane = lax.broadcasted_iota(jnp.int32, (224, 128), 1)
-        bit = lax.broadcasted_iota(jnp.int32, (LOW, 128), 1) % 16
-        for j in range(4):
-            spread = (block == (g * 4 + j) * 8 + lane // 16).astype(f32).astype(jnp.bfloat16)
-            high = jnp.dot(upper, spread, preferred_element_type=f32)
-            low = jnp.dot(lower, spread, preferred_element_type=f32)
-            word = (high * 256.0 + low).astype(jnp.int32)
-            mask[g, j] = (jnp.right_shift(word, bit) & 1).astype(f32)
-        return carry
-
-    lax.fori_loop(0, GROUPS, group_mask, 0)
+    def kept_copy():
+        return pltpu.make_async_remote_copy(
+            src_ref=keptb, dst_ref=kept_far, send_sem=k_sem.at[0], recv_sem=k_sem.at[1],
+            device_id=along_z(jnp.where(z_lo == 1, 1, 3)), device_id_type=MESH)
 
     mine = pl.ds(pl.multiple_of(x * PIECE, 8), PIECE)
 
@@ -268,7 +339,89 @@
         z3_copy(g, 0).start()
         return carry
 
-    lax.fori_loop(0, GROUPS, sum_plane, 0)
+    def gather_chip(packed, g, carry):
+        for j in range(4):
+            @pl.when(4 * g + j + 1 < CHUNKS)
+            def _():
+                send_stage(4 * g + j + 1)
+            process(g, j, packed)
+            if packed and j % 2 == 1:
+                pack_pair(g, j - 1)
+        if not packed:
+            @pl.when(g == 0)
+            def _():
+                meet_plane()
+                kept_copy().start()
+        rs_send(g)
+        if packed:
+            pl.when(g >= 2)(lambda: sum_plane(g - 2, None))
+        return carry
+
+    lax.fori_loop(0, RAW, functools.partial(gather_chip, False), 0)
+    r, c = (lax.broadcasted_iota(jnp.int32, (128, 128), n) for n in (0, 1))
+    same[...] = (r // 16 == c // 16).astype(f32).astype(jnp.bfloat16)
+    before[...] = ((r // 16 == c // 16) & (r < c)).astype(f32).astype(jnp.bfloat16)
+    r, c = (lax.broadcasted_iota(jnp.int32, (LOW, LOW), n) for n in (0, 1))
+    above[...] = ((r // 32 == c // 32) & (r % 2 == c % 2) & (c < r)).astype(f32).astype(jnp.bfloat16)
+
+    unpack_words(rowbits, keptb)
+
+    def group_mask(g, carry):
+        for j in range(4):
+            mask[g, j] = kept_mask(rowbits, 4 * g + j).astype(f32)
+        return carry
+
+    def group_moves(g, carry):
+        for pair in (0, 2):
+            _, given = moves([mask[g, pair + n].astype(jnp.int32) for n in (0, 1)])
+            for n in (0, 1):
+                gives_of[g, pair + n] = given[n]
+        return carry
+
+    lax.fori_loop(0, GROUPS, group_mask, 0)
+    lax.fori_loop(RAW, MOVES, group_moves, 0)
+    kept_copy().wait_recv()
+    unpack_words(words_far, kept_far)
+    lax.fori_loop(RAW, GROUPS, functools.partial(gather_chip, True), 0)
+
+    def moment_copy(c):
+        return pltpu.make_async_copy(own.at[c], moment_out.at[0, :, columns(c)], om_sem.at[c])
+
+    def finish_raw(g, carry):
+        for j in range(4):
+            c = 4 * g + j
+            z_copy(c, HALF).wait_recv()
+            moment = own[c] + jnp.concatenate([zrecv[c, :ROWS], zrecv[c, ROWS:]], axis=1)
+            own[c] = moment - inverse(mask[g, j] * forward(moment))
+            moment_copy(c).start()
+        return carry
+
+    def finish(g, carry):
+        fill = jnp.zeros((8, 128), f32)
+        for pair in (0, 2):
+            kept_here = [mask[g, pair + n].astype(jnp.int32) for n in (0, 1)]
+            given = [gives_of[g, pair + n] for n in (0, 1)]
+            packed = []
+            for n in (0, 1):
+                c = 4 * g + pair + n
+                z_copy(c, PACKED).wait_recv()
+                top = ROWS + LOW
+                packed.append(jnp.concatenate(
+                    [zrecv[c, top:top + 24], fill, zrecv[c, top + 24:top + 48], fill, zrecv[c, top + 48:top + 72], fill],
+                    axis=0))
+            others = unpack(packed, given)
+            for n in (0, 1):
+                c = 4 * g + pair + n
+                low = jnp.where(kept_here[n] == 1, -cf[g, 0, pair + n], others[n])
+                wide = split_dot(jnp.concatenate([low, zrecv[c, ROWS:ROWS + LOW]], axis=1), (right_t[0], right_t[1]))
+                high = jnp.concatenate([zrecv[c, :LOW], zrecv[c, LOW:ROWS]], axis=1)
+                both = jnp.concatenate([wide, high], axis=0)
+                own[c] = own[c] + split_dot((left_t[0], left_t[1]), both)
+                moment_copy(c).start()
+        return carry
+
+    lax.fori_loop(GROUPS - 2, GROUPS, sum_plane, 0)
+    lax.fori_loop(0, RAW, finish_raw, 0)
 
     def sum_pair(g, carry):
         z3_copy(g, 0).wait_recv()
@@ -279,10 +432,11 @@
     lax.fori_loop(0, GROUPS, sum_pair, 0)
 
     def start_z(c, carry):
-        z_copy(c).start()
+        z_copy(c, PACKED).start()
         return carry
 
     lax.fori_loop(EARLY, CHUNKS, start_z, 0)
+    lax.fori_loop(RAW, AHEAD, finish, 0)
 
     def sum_z(g, carry):
         z3_copy(g, 1).wait_recv()
@@ -300,6 +454,7 @@
 
     lax.fori_loop(0, GROUPS, sum_z, 0)
 
+
     def agg_copy(c):
         return pltpu.make_async_copy(mombuf.at[c], agg_out.at[:, columns(c)], oa_sem.at[c])
 
@@ -308,43 +463,27 @@
 
     def expand_mean(g, carry):
         pltpu.make_async_copy(rsr.at[g, :, 0], rsr.at[g, :, 0], ag_r.at[g]).wait()
-        for half in (0, 1):
-            c = 2 * g + half
+        for j in range(4):
+            c = 4 * g + j
             load_weight(c).wait()
-            for h in (0, 1):
-                j = 2 * half + h
-                wide = slice(256 * h, 256 * h + 256)
-                agg = inverse(mask[g, j] * (mean[g, j] / 32.0))
-                mombuf[c, :, wide] = agg
-                wbuf[c, :, wide] = (wbuf[c, :, wide].astype(f32) - step_rate * agg).astype(jnp.bfloat16)
+            agg = inverse(mask[g, j] * (mean[g, j] / 32.0))
+            mombuf[c] = agg
+            wbuf[c] = (wbuf[c].astype(f32) - step_rate * agg).astype(jnp.bfloat16)
             agg_copy(c).start()
             new_weight_copy(c).start()
         return carry
 
+    lax.fori_loop(MOVES, GROUPS, group_moves, 0)
+    lax.fori_loop(AHEAD, MIDDLE, finish, 0)
     lax.fori_loop(0, GROUPS, expand_mean, 0)
 
-    def moment_copy(c):
-        return pltpu.make_async_copy(zrecv.at[c], moment_out.at[0, :, columns(c)], om_sem.at[c])
-
-    def finish(g, carry):
-        for half in (0, 1):
-            c = 2 * g + half
-            z_copy(c).wait_recv()
-            for h in (0, 1):
-                wide = slice(256 * h, 256 * h + 256)
-                moment = sib[1, c, :, wide] + zrecv[c, :, wide]
-                zrecv[c, :, wide] = moment - inverse(mask[g, 2 * half + h] * forward(moment))
-            moment_copy(c).start()
-        return carry
-
-    lax.fori_loop(0, GROUPS, finish, 0)
+    lax.fori_loop(MIDDLE, GROUPS, finish, 0)
 
     for c in range(CHUNKS - SLOTS, CHUNKS):
         for n in (0, 1):
             sib_copy(c, n).wait_send()
 
     def drain_chunk(c, carry):
-        z_copy(c).wait_send()
         agg_copy(c).wait()
         new_weight_copy(c).wait()
         moment_copy(c).wait()
@@ -359,6 +498,14 @@
 
     lax.fori_loop(0, GROUPS, drain_group, 0)
     lax.fori_loop(0, CHUNKS, drain_chunk, 0)
+
+    def drain_z(rows, c, carry):
+        z_copy(c, rows).wait_send()
+        return carry
+
+    lax.fori_loop(0, 4 * RAW, functools.partial(drain_z, HALF), 0)
+    lax.fori_loop(4 * RAW, CHUNKS, functools.partial(drain_z, PACKED), 0)
+    kept_copy().wait_send()
 
 
 def write_out(*refs):
@@ -377,7 +524,7 @@
 
 
 def per_device(partials, momentum, weight, kept):
-    left, right, left_t, right_t = (jnp.asarray(t) for t in low_tables())
+    left, right, left_t, right_t = (jnp.asarray(t) for t in tables())
     f32, bf16, i32 = jnp.float32, jnp.bfloat16, jnp.int32
     dma = pltpu.SemaphoreType.DMA
     vmem = pltpu.VMEM
@@ -393,9 +540,11 @@
         out_specs=(hbm,) * 3,
         scratch_shapes=[
             vmem((LOADS, 4, ROWS, CHUNK), bf16),
-            vmem((SLOTS, 2, ROWS, CHUNK), f32),
-            vmem((2, CHUNKS, ROWS, CHUNK), f32),
+            vmem((SLOTS, ROWS, CHUNK), f32),
+            vmem((SLOTS, HALF, 128), f32),
             vmem((CHUNKS, ROWS, CHUNK), f32),
+            vmem((CHUNKS, HALF, 128), f32),
+            vmem((CHUNKS, HALF, 128), f32),
             vmem((CHUNKS, ROWS, CHUNK), f32),
             vmem((CHUNKS, ROWS, CHUNK), bf16),
             vmem((GROUPS, 2, 4, LOW, 128), f32),
@@ -405,23 +554,29 @@
             vmem((GROUPS, 4, LOW, 128), f32),
             vmem((GROUPS, 4, LOW, 128), f32),
             vmem((6, 64, 224), i32),
-            vmem((6, 16, 224), i32),
-            vmem((LOW, ROWS), f32),
-            vmem((256, 128), f32),
-            vmem((ROWS, LOW), f32),
-            vmem((128, 256), f32),
-            vmem((2, LOW, ROWS), bf16),
-            vmem((2, 256, 128), bf16),
-            vmem((2, ROWS, LOW), bf16),
-            vmem((2, 128, 256), bf16),
+            vmem((3, 32, 224), i32),
+            vmem((6, 64, 224), i32),
+            vmem((3, 32, 224), i32),
+            vmem((GROUPS, 4, LOW, 128), i32),
+            vmem((128, 128), bf16),
+            vmem((128, 128), bf16),
+            vmem((LOW, LOW), bf16),
+            vmem((ROWS, ROWS), f32),
+            vmem((256, 256), f32),
+            vmem((ROWS, ROWS), f32),
+            vmem((256, 256), f32),
+            vmem((2, ROWS, ROWS), bf16),
+            vmem((2, 256, 256), bf16),
+            vmem((2, ROWS, ROWS), bf16),
+            vmem((2, 256, 256), bf16),
             dma((5,)), dma((LOADS,)), dma((CHUNKS,)), dma((CHUNKS,)),
             dma((SLOTS, 2)), dma((CHUNKS, 2)), dma((CHUNKS,)), dma((CHUNKS,)),
             dma((GROUPS,)), dma((GROUPS,)), dma((GROUPS, 2)), dma((GROUPS, 2)), dma((GROUPS,)), dma((GROUPS,)),
             dma((CHUNKS,)), dma((CHUNKS,)), dma((CHUNKS,)),
-            pltpu.SemaphoreType.REGULAR, pltpu.SemaphoreType.REGULAR,
+            dma((2,)), pltpu.SemaphoreType.REGULAR, pltpu.SemaphoreType.REGULAR,
         ],
         compiler_params=pltpu.CompilerParams(
-            collective_id=0, has_side_effects=True, vmem_limit_bytes=46 * 2 ** 20),
+            collective_id=0, has_side_effects=True, vmem_limit_bytes=48 * 2 ** 20),
         cost_estimate=pl.CostEstimate(flops=8 * 10 ** 9, bytes_accessed=34 * 10 ** 6, transcendentals=0),
         name="compress_step",
     )(partials, momentum, weight, jnp.transpose(kept, (0, 2, 1)), left, right, left_t, right_t)

time: 136 us -> 132 us (0.971)
  Pallas kernels: 135 us -> 131 us
    pallas_call x1, Pallas kernels: 130 us -> 126 us  [per_device(): pl.pallas_call(kernel, out_shape=(vmem((1, ROWS, QUARTER), f32), vmem((RO...]
where the time goes in v4:
time: 132 us
  Pallas kernels  131 us (99%)
    pallas_call x1, Pallas kernels, per_device(): pl.pallas_call(kernel, out_shape=(vmem((1, ROWS, QUARTER), f32), vmem((RO...  126 us
    pallas_call x1, Pallas kernels, per_device(): pl.pallas_call(write_out, out_shape=tuple((jax.ShapeDtypeStruct(r.shape,...  5.06 us

profile of v4, /device:TPU:0, one launch (start us, length us, event | category | flops | bytes accessed | tf_op | source)
XLA Modules:
  0.0 131.9 jit_solution(4623555296202148055)
XLA Ops:
  0.6 126.0 %compress_step.1 = (f32[1,192,7168]{2,1,0:T(8,128)S(1)}, f32[192,7168]{1,0:T(8,128)S(1)}, bf16[192,7168]{1,0:T(8,128)(2,1)S(1)}) custom-call(bf16[1,1,192,28672]{3,2,1,0:T(8,128)(2,1)} %part.1, f32[1,192,7168]{2,1,0:T(8,128)} %mom.1, bf16[192,7168]{1,0:T(8,128)(2,1)} %wt.1, s32[6,64,224]{2,1,0:T(8,128)} %bitcast.1, f32[192,192]{1,0:T(8,128)} %constant.8.clone.left_in, ...), custom_call_target="tpu_custom_call" | custom-call | flops 8000000000 | bytes 34000000 | tf_op jit(solution)/shard_map/compress_step/pallas_call | solution.py:532
  126.6 5.1 %write_out.1 = (f32[1,192,7168]{2,1,0:T(8,128)}, f32[192,7168]{1,0:T(8,128)}, bf16[192,7168]{1,0:T(8,128)(2,1)}) custom-call(f32[1,192,7168]{2,1,0:T(8,128)S(1)} %get-tuple-element.6.refs_0_, f32[192,7168]{1,0:T(8,128)S(1)} %get-tuple-element.7.refs_1_, bf16[192,7168]{1,0:T(8,128)(2,1)S(1)} %get-tuple-element.8.refs_2_), custom_call_target="tpu_custom_call" | custom-call | tf_op jit(solution)/shard_map/write_out/pallas_call | solution.py:583

commit v5 on v4

--- a/solution.py
+++ b/solution.py
@@ -27,7 +27,7 @@
 RAW = 2
 HALF = 2 * ROWS
 PACKED = 360
-EARLY = 20
+EARLY = 16
 
 
 def tables():
@@ -112,8 +112,11 @@
             copy.start()
         return carry
 
-    def start_rest(c, carry):
+    def start_mom(c, carry):
         load_mom(c).start()
+        return carry
+
+    def start_weight(c, carry):
         load_weight(c).start()
         return carry
 
@@ -262,15 +265,13 @@
 
     def process(g, j, packed):
         c = 4 * g + j
-        sib_copy(c, 0).wait_recv()
-        mine_far = pbuf[c % LOADS, 2].astype(f32)
-        chip = jnp.concatenate([far[c, :ROWS] + mine_far[:, :128], far[c, ROWS:] + mine_far[:, 128:]], axis=1)
         if not packed:
-            far[c, :ROWS] = chip[:, :128]
-            far[c, ROWS:] = chip[:, 128:]
-            z_copy(c, HALF).start()
-            cf[g, 1, j] = forward(chip)
+            pl.when(c > 0)(lambda: raw_send(c))
+            cf[g, 1, j] = forward(jnp.concatenate([far[c, :ROWS], far[c, ROWS:]], axis=1))
         else:
+            sib_copy(c, 0).wait_recv()
+            mine_far = pbuf[c % LOADS, 2].astype(f32)
+            chip = jnp.concatenate([far[c, :ROWS] + mine_far[:, :128], far[c, ROWS:] + mine_far[:, 128:]], axis=1)
             lefted = split_dot((left[0], left[1]), chip)
             righted = split_dot(lefted[:LOW], (right[0], right[1]))
             cf[g, 1, j] = righted[:, :128]
@@ -303,11 +304,21 @@
             return carry
         lax.fori_loop(1, 16, one, 0)
 
+    def raw_send(c):
+        sib_copy(c, 0).wait_recv()
+        mine_far = pbuf[c % LOADS, 2].astype(f32)
+        far[c, :ROWS] = far[c, :ROWS] + mine_far[:, :128]
+        far[c, ROWS:] = far[c, ROWS:] + mine_far[:, 128:]
+        z_copy(c, HALF).start()
+
     send_stage(0)
+    start_part(1, 0)
+    start_part(2, 0)
     for copy in consts:
         copy.start()
-    lax.fori_loop(1, LOADS, start_part, 0)
-    lax.fori_loop(0, CHUNKS, start_rest, 0)
+    raw_send(0)
+    lax.fori_loop(3, LOADS, start_part, 0)
+    lax.fori_loop(0, CHUNKS, start_mom, 0)
     for copy in consts:
         copy.wait()
     for whole, pair in ((left32, left), (right32, right), (left_t32, left_t), (right_t32, right_t)):
@@ -378,6 +389,7 @@
                 gives_of[g, pair + n] = given[n]
         return carry
 
+    lax.fori_loop(0, CHUNKS, start_weight, 0)
     lax.fori_loop(0, GROUPS, group_mask, 0)
     lax.fori_loop(RAW, MOVES, group_moves, 0)
     kept_copy().wait_recv()
@@ -396,23 +408,23 @@
             moment_copy(c).start()
         return carry
 
-    def finish(g, carry):
+    def finish(g, carry, sets=((0, 1), (2, 3))):
         fill = jnp.zeros((8, 128), f32)
-        for pair in (0, 2):
-            kept_here = [mask[g, pair + n].astype(jnp.int32) for n in (0, 1)]
-            given = [gives_of[g, pair + n] for n in (0, 1)]
+        for js in sets:
+            kept_here = [mask[g, j].astype(jnp.int32) for j in js]
+            given = [gives_of[g, j] for j in js]
             packed = []
-            for n in (0, 1):
-                c = 4 * g + pair + n
+            for j in js:
+                c = 4 * g + j
                 z_copy(c, PACKED).wait_recv()
                 top = ROWS + LOW
                 packed.append(jnp.concatenate(
                     [zrecv[c, top:top + 24], fill, zrecv[c, top + 24:top + 48], fill, zrecv[c, top + 48:top + 72], fill],
                     axis=0))
             others = unpack(packed, given)
-            for n in (0, 1):
-                c = 4 * g + pair + n
-                low = jnp.where(kept_here[n] == 1, -cf[g, 0, pair + n], others[n])
+            for n, j in enumerate(js):
+                c = 4 * g + j
+                low = jnp.where(kept_here[n] == 1, -cf[g, 0, j], others[n])
                 wide = split_dot(jnp.concatenate([low, zrecv[c, ROWS:ROWS + LOW]], axis=1), (right_t[0], right_t[1]))
                 high = jnp.concatenate([zrecv[c, :LOW], zrecv[c, LOW:ROWS]], axis=1)
                 both = jnp.concatenate([wide, high], axis=0)
@@ -421,7 +433,7 @@
         return carry
 
     lax.fori_loop(GROUPS - 2, GROUPS, sum_plane, 0)
-    lax.fori_loop(0, RAW, finish_raw, 0)
+    lax.fori_loop(0, 1, finish_raw, 0)
 
     def sum_pair(g, carry):
         z3_copy(g, 0).wait_recv()
@@ -436,6 +448,7 @@
         return carry
 
     lax.fori_loop(EARLY, CHUNKS, start_z, 0)
+    lax.fori_loop(1, RAW, finish_raw, 0)
     lax.fori_loop(RAW, AHEAD, finish, 0)
 
     def sum_z(g, carry):
@@ -477,16 +490,16 @@
     lax.fori_loop(AHEAD, MIDDLE, finish, 0)
     lax.fori_loop(0, GROUPS, expand_mean, 0)
 
-    lax.fori_loop(MIDDLE, GROUPS, finish, 0)
-
-    for c in range(CHUNKS - SLOTS, CHUNKS):
+    lax.fori_loop(MIDDLE, GROUPS - 1, finish, 0)
+
+    def drain_sib(c, carry):
         for n in (0, 1):
             sib_copy(c, n).wait_send()
-
-    def drain_chunk(c, carry):
+        return carry
+
+    def drain_agg(c, carry):
         agg_copy(c).wait()
         new_weight_copy(c).wait()
-        moment_copy(c).wait()
         return carry
 
     def drain_group(g, carry):
@@ -496,16 +509,19 @@
             z3_copy(g, step).wait_send()
         return carry
 
+    def drain_moment(rows, c, carry):
+        z_copy(c, rows).wait_send()
+        moment_copy(c).wait()
+        return carry
+
+    kept_copy().wait_send()
+    lax.fori_loop(CHUNKS - SLOTS, CHUNKS, drain_sib, 0)
     lax.fori_loop(0, GROUPS, drain_group, 0)
-    lax.fori_loop(0, CHUNKS, drain_chunk, 0)
-
-    def drain_z(rows, c, carry):
-        z_copy(c, rows).wait_send()
-        return carry
-
-    lax.fori_loop(0, 4 * RAW, functools.partial(drain_z, HALF), 0)
-    lax.fori_loop(4 * RAW, CHUNKS, functools.partial(drain_z, PACKED), 0)
-    kept_copy().wait_send()
+    lax.fori_loop(0, CHUNKS, drain_agg, 0)
+    lax.fori_loop(0, 4 * RAW, functools.partial(drain_moment, HALF), 0)
+    lax.fori_loop(4 * RAW, CHUNKS - 4, functools.partial(drain_moment, PACKED), 0)
+    finish(GROUPS - 1, 0, ((0, 1), (2,), (3,)))
+    lax.fori_loop(CHUNKS - 4, CHUNKS, functools.partial(drain_moment, PACKED), 0)
 
 
 def write_out(*refs):

time: 132 us -> 130 us (0.985)
  Pallas kernels: 131 us -> 129 us
    pallas_call x1, Pallas kernels: 126 us -> 124 us  [per_device(): pl.pallas_call(kernel, out_shape=(vmem((1, ROWS, QUARTER), f32), vmem((RO...]
where the time goes in v5:
time: 130 us
  Pallas kernels  129 us (99%)
    pallas_call x1, Pallas kernels, per_device(): pl.pallas_call(kernel, out_shape=(vmem((1, ROWS, QUARTER), f32), vmem((RO...  124 us
    pallas_call x1, Pallas kernels, per_device(): pl.pallas_call(write_out, out_shape=tuple((jax.ShapeDtypeStruct(r.shape,...  5.06 us

profile of v5, /device:TPU:0, one launch (start us, length us, event | category | flops | bytes accessed | tf_op | source)
XLA Modules:
  0.0 130.1 jit_solution(7109203358346264621)
XLA Ops:
  0.6 124.2 %compress_step.1 = (f32[1,192,7168]{2,1,0:T(8,128)S(1)}, f32[192,7168]{1,0:T(8,128)S(1)}, bf16[192,7168]{1,0:T(8,128)(2,1)S(1)}) custom-call(bf16[1,1,192,28672]{3,2,1,0:T(8,128)(2,1)} %part.1, f32[1,192,7168]{2,1,0:T(8,128)} %mom.1, bf16[192,7168]{1,0:T(8,128)(2,1)} %wt.1, s32[6,64,224]{2,1,0:T(8,128)} %bitcast.1, f32[192,192]{1,0:T(8,128)} %constant.8.clone.left_in, ...), custom_call_target="tpu_custom_call" | custom-call | flops 8000000000 | bytes 34000000 | tf_op jit(solution)/shard_map/compress_step/pallas_call | solution.py:548
  124.9 5.1 %write_out.1 = (f32[1,192,7168]{2,1,0:T(8,128)}, f32[192,7168]{1,0:T(8,128)}, bf16[192,7168]{1,0:T(8,128)(2,1)}) custom-call(f32[1,192,7168]{2,1,0:T(8,128)S(1)} %get-tuple-element.6.refs_0_, f32[192,7168]{1,0:T(8,128)S(1)} %get-tuple-element.7.refs_1_, bf16[192,7168]{1,0:T(8,128)(2,1)S(1)} %get-tuple-element.8.refs_2_), custom_call_target="tpu_custom_call" | custom-call | tf_op jit(solution)/shard_map/write_out/pallas_call | solution.py:599
